TPU v7x, 256 devices: a whole 4x4x8 slice. The times are simulated.
256 devices in a mesh: replica: 16 (over z, y_lo), fsdp: 16 (over y_hi, x, core).
Axes of the slice: x: 4, y: 4 (y_hi: 2, y_lo: 2; y = y_hi * 2 + y_lo), z: 8, core: 2. Of those that a mesh axis runs over, the one named last changes fastest.
Arguments:
- tokens: bfloat16 [16, 8192, 4608], P('replica', 'fsdp'), may hold values from -6 to 6
- targets: bfloat16 [16, 8192, 1024], P('replica', 'fsdp'), may hold values from -6 to 6
- local_weights: bfloat16 [16, 4608, 1024], P('replica', 'fsdp'), may hold values from -5 to 5, as said below
- first_moment: float32 [16, 4608, 1024], P('replica', 'fsdp'), may hold values from -6 to 6
- second_moment: float32 [16, 4608, 1024], P('replica', 'fsdp'), may hold values from 0.5 to 4
- global_weights: float32 [4608, 1024], P('fsdp'), may hold values from -4 to 4
- outer_momentum: float32 [4608, 1024], P('fsdp'), may hold values from -0.6 to 0.6
Outputs:
- new_local: bfloat16 [16, 4608, 1024], P('replica', 'fsdp')
- new_first: float32 [16, 4608, 1024], P('replica', 'fsdp')
- new_second: float32 [16, 4608, 1024], P('replica', 'fsdp')
- new_global: float32 [4608, 1024], P('fsdp')
- new_momentum: float32 [4608, 1024], P('fsdp')
Inputs may be any that keep to these rules, and one draw needn't show every extreme that they name: `local_weights`: each replica's weights lie near global_weights.
All inputs are finite; a program needn't handle non-finite values.
Results may differ from a plain program's by a relative error of at most 0.024.
Values may be sent and summed in bfloat16 or wider, within the bound.
No kernel may reach another device: no remote copies, remote signals or barrier semaphores. Data moves between devices by JAX's collectives and lax.ppermute only.
A program may use at most 128 MiB of HBM per device.

v0:
```python
import math

import jax
import jax.numpy as jnp
from jax import lax
from jax.sharding import PartitionSpec as P

inner_rate = 0.02
first_decay = 0.5
second_decay = 0.95
adam_eps = 1e-08
weight_decay = 0.1
outer_rate = 0.7
outer_mu = 0.9
mix_keep = 0.5


def local(
    tokens, targets, local_weights, first_moment, second_moment, global_weights, outer_momentum
):
    rows = tokens[0]
    wanted = targets[0]
    weight = local_weights[0]
    first = first_moment[0]
    second = second_moment[0]
    tok_rows = rows.shape[0]
    width = rows.shape[1]
    total_rows = tok_rows * lax.axis_size("fsdp")
    out_scale = 1.0 / math.sqrt(width)
    grad_scale = 1.0 / math.sqrt(total_rows)
    contract_rows = (((0,), (0,)), ((), ()))
    columns = rows
    projected = (
        jnp.dot(
            columns,
            lax.all_gather(weight, "fsdp", axis=0, tiled=True),
            preferred_element_type=jnp.float32,
        )
        * out_scale
    )
    residual = (projected - wanted.astype(jnp.float32)).astype(jnp.bfloat16)
    columns = rows
    term = lax.dot_general(columns, residual, contract_rows, preferred_element_type=jnp.float32)
    grad = lax.psum_scatter(
        term.astype(jnp.bfloat16).astype(jnp.float32).astype(jnp.bfloat16),
        "fsdp",
        scatter_dimension=0,
        tiled=True,
    ).astype(jnp.float32)
    grad = grad * grad_scale
    first = first_decay * first + (1.0 - first_decay) * grad
    second = second_decay * second + (1.0 - second_decay) * grad * grad
    wide = weight.astype(jnp.float32)
    weight = (
        wide - inner_rate * (first / (jnp.sqrt(second) + adam_eps) + weight_decay * wide)
    ).astype(jnp.bfloat16)
    delta = (global_weights - weight.astype(jnp.float32)).astype(jnp.bfloat16)
    total = lax.psum(delta.astype(jnp.float32).astype(jnp.bfloat16), "replica").astype(jnp.float32)
    mean = total / lax.axis_size("replica")
    new_momentum = outer_mu * outer_momentum + mean
    new_global = global_weights - outer_rate * (mean + outer_mu * new_momentum)
    new_local = (mix_keep * weight.astype(jnp.float32) + (1.0 - mix_keep) * new_global).astype(
        jnp.bfloat16
    )
    return (new_local[None], first[None], second[None], new_global, new_momentum)


def solution(mesh):
    return jax.shard_map(
        local,
        mesh=mesh,
        in_specs=(
            P("replica", "fsdp", None),
            P("replica", "fsdp", None),
            P("replica", "fsdp", None),
            P("replica", "fsdp", None),
            P("replica", "fsdp", None),
            P("fsdp", None),
            P("fsdp", None),
        ),
        out_specs=(
            P("replica", "fsdp", None),
            P("replica", "fsdp", None),
            P("replica", "fsdp", None),
            P("fsdp", None),
            P("fsdp", None),
        ),
        check_vma=False,
    )
```

profile of v0, /device:TPU:2, one launch (start us, length us, event | category | flops | bytes accessed | tf_op | source)
XLA Modules:
  0.0 401.4 jit_solution(16362465706857808088)
XLA Ops:
  7.2 0.0 all-gather.3.cloned.1.call-start
  7.2 0.7 all-gather.3.cloned.1.call-update
  7.9 0.0 reduce-scatter.4.cloned.1.call-start
  7.9 86.7 %all-gather.3.cloned.1.call-done = bf16[1,4608,1024]{2,1,0:T(8,128)(2,1)} async-done(((bf16[1,288,1024]{2,1,0:T(8,128)(2,1)}), bf16[1,4608,1024]{2,1,0:T(8,128)(2,1)}) %all-gather.3.cloned.1.call-update) | async-done | bytes 9437200 | tf_op jit(solution)/shard_map/all_gather | solution.py:36
  94.7 9.2 %fusion.5 = bf16[512,1024]{1,0:T(8,128)(2,1)S(1)} fusion(bf16[1,4608,1024]{2,1,0:T(8,128)(2,1)} %all-gather.3.cloned.1.call-done, bf16[1,512,4608]{2,1,0:T(8,128)(2,1)} %param.7, bf16[1,512,1024]{2,1,0:T(8,128)(2,1)} %param.8), kind=kOutput, calls=%fused_computation.10 | convolution fusion | flops 4833935360 | bytes 16252928 | tf_op jit(solution)/shard_map/dot_general | solution.py:34
  103.8 9.8 %fusion.2 = bf16[4608,1024]{0,1:T(8,128)(2,1)} fusion(bf16[512,1024]{1,0:T(8,128)(2,1)S(1)} %fusion.5, bf16[1,512,4608]{2,1,0:T(8,128)(2,1)} %param.7), kind=kOutput, calls=%fused_computation.3 | convolution fusion | flops 4836556800 | bytes 15204352 | tf_op jit(solution)/shard_map/dot_general | solution.py:43
  113.7 12.7 %copy.34 = bf16[4608,1024]{1,0:T(8,128)(2,1)} copy(bf16[4608,1024]{0,1:T(8,128)(2,1)} %fusion.2) | data formatting | bytes 18874368
  126.4 0.0 all-reduce.2.cloned.1.call-start
  126.5 1.0 copy-done.1
  127.5 1.2 copy.23
  128.6 0.5 copy.28
  129.1 3.0 copy.24
  132.1 1.6 copy.25
  133.7 106.8 %reduce-scatter.4.cloned.1.call-done = bf16[288,1024]{1,0:T(8,128)(2,1)} async-done(((bf16[4608,1024]{1,0:T(8,128)(2,1)}), bf16[288,1024]{1,0:T(8,128)(2,1)}) %reduce-scatter.4.cloned.1.call-update) | async-done | bytes 589840
  240.5 2.2 copy.35
  242.7 5.5 %fusion.10 = (bf16[288,1024]{0,1:T(8,128)(2,1)}, bf16[288,1024]{0,1:T(8,128)(2,1)}, f32[1,288,1024]{1,2,0:T(8,128)S(1)}, f32[1,288,1024]{1,2,0:T(8,128)}) fusion(f32[288,1024]{0,1:T(8,128)S(1)} %copy.28, f32[1,288,1024]{1,2,0:T(8,128)} %copy.25, bf16[288,1024]{0,1:T(8,128)(2,1)} %copy.35, f32[1,288,1024]{1,2,0:T(8,128)} %copy.24, bf16[1,288,1024]{1,2,0:T(8,128)(2,1)} %copy.23), kind=kLoop, calls=%fused_computation.15 | loop fusion | flops 5898240 | bytes 8257536 | tf_op jit(solution)/shard_map/convert_element_type | solution.py:57
  248.2 2.9 copy.27
  251.1 2.9 copy.30
  254.0 1.5 copy.31
  255.5 130.2 %all-reduce.2.cloned.1.call-done = bf16[288,1024]{0,1:T(8,128)(2,1)} async-done(((bf16[288,1024]{0,1:T(8,128)(2,1)}), bf16[288,1024]{0,1:T(8,128)(2,1)}) %all-reduce.2.cloned.1.call-update) | async-done | bytes 589840 | tf_op jit(solution)/shard_map/psum | solution.py:58
  385.7 3.8 fusion.20
  389.5 2.9 copy.32
  392.3 1.5 copy.33
  393.8 1.1 copy.29
  (9 shorter events, 0.1 us)
Async XLA Ops:
  7.2 87.5 %all-gather.3.cloned.1.call-start = ((), (), s32[]{:S(2)}) async-start(), calls=%async_computation.2 | async-start | bytes 10027008 | tf_op jit(solution)/shard_map/all_gather | solution.py:36
  7.9 232.6 %reduce-scatter.4.cloned.1.call-start = ((), (), s32[]{:S(2)}) async-start(), calls=%async_computation.3 | async-start | bytes 10027008
  126.4 1.1 copy-start.1
  126.4 2.2 copy-start.2
  126.4 259.2 %all-reduce.2.cloned.1.call-start = ((), (), s32[]{:S(2)}) async-start(), calls=%async_computation.1 | async-start | bytes 1572864 | tf_op jit(solution)/shard_map/psum | solution.py:58
  129.1 3.0 copy-start.3
  392.3 1.5 copy-start
Sparse Core Ops, SparseCore 0:
  10.7 83.9 all-gather.2
  126.5 113.9 reduce-scatter.3
  248.4 137.2 all-reduce.1
where the time goes:
time: 402 us; the launch traced here: 401 us
  waiting for transfers between devices  324 us (81%)
  local copies, waits for them, and re-layouts  34.8 us (9%)
  matrix products  19 us (5%)
  between operations  13.8 us (3%)
  other arithmetic  9.3 us (2%)
    psum x1, waiting for transfers between devices, local(): lax.psum(delta.astype(jnp.float32).astype(jnp.bfloat16), 'replica')  130 us
    unnamed x4, waiting for transfers between devices  108 us
    all_gather x1, waiting for transfers between devices, local(): lax.all_gather(weight, 'fsdp', axis=0, tiled=True)  86.7 us
    unnamed x20, local copies, waits for them, and re-layouts  34.8 us
    dot_general x1, matrix products, local(): lax.dot_general(columns, residual, contract_rows, preferred_element_type=...  9.83 us
    dot_general x1, matrix products, local(): jnp.dot(columns, lax.all_gather(weight, 'fsdp', axis=0, tiled=True), pref...  9.17 us
  transfers between devices with their start and end apart: 3, of which 3 were waited for; matrix products, arithmetic and copies ran while one was open for 3% of the time, Pallas kernels for 0%

commit v1 on v0

v1 whole, which is shorter than its diff:
```python
import math

import jax
import jax.numpy as jnp
from jax import lax
from jax.experimental import pallas as pl
from jax.experimental.pallas import tpu as pltpu
from jax.sharding import PartitionSpec as P

inner_rate = 0.02
first_decay = 0.5
second_decay = 0.95
adam_eps = 1e-08
weight_decay = 0.1
outer_rate = 0.7
outer_mu = 0.9
mix_keep = 0.5

BF = jnp.bfloat16
F32 = jnp.float32

D = 4608
KVW = 1024
TOK = 512
UNIT = 288
PART = 96
QUAD = 4 * PART
HALF = 2304
REPLICAS = 16
MIB = 1024 * 1024

EVEN, ODD, WIDE = 0, 1, 2
ORDERS = ((EVEN, ODD, WIDE), (ODD, WIDE, EVEN), (WIDE, EVEN, ODD))
FLIP = {EVEN: 2, ODD: 6, WIDE: 8}
SWAP_CORE = [(i, i ^ 1) for i in range(16)]


def chip_bit(chip, dim):
    x = chip % 4
    if dim == EVEN:
        return (x ^ (x // 2)) % 2
    if dim == ODD:
        return x // 2
    return chip // 4


def unit_order(part):
    one, two, three = ORDERS[part]
    return sorted(
        range(8), key=lambda chip: (chip_bit(chip, three), chip_bit(chip, two), chip_bit(chip, one))
    )


def own_bits():
    me = lax.axis_index("fsdp")
    x = (me >> 1) & 3
    return {EVEN: (x ^ (x >> 1)) & 1, ODD: x >> 1, WIDE: me >> 3}, me & 1


def flip(value, dim):
    return lax.ppermute(value, "fsdp", [(i, i ^ FLIP[dim]) for i in range(16)])


def swap(value):
    return lax.ppermute(value, "fsdp", SWAP_CORE)


def params(mib):
    return pltpu.CompilerParams(vmem_limit_bytes=mib * MIB)


def cost(flops, nbytes):
    return pl.CostEstimate(flops=flops, bytes_accessed=nbytes, transcendentals=0)


def pack_kernel(core_ref, rows_ref, keep_ref, send_ref):
    rows = rows_ref[...]

    def packed(core):
        pieces = []
        for part in range(3):
            for chip in unit_order(part):
                at = 2 * UNIT * chip + UNIT * core + PART * part
                pieces.append(rows[:, at : at + PART])
        return jnp.concatenate(pieces, axis=1)

    zero = packed(0)
    one = packed(1)

    @pl.when(core_ref[0] == 0)
    def _():
        keep_ref[...] = zero
        send_ref[...] = one

    @pl.when(core_ref[0] == 1)
    def _():
        keep_ref[...] = one
        send_ref[...] = zero


def pack(core, rows):
    tile = 128
    return pl.pallas_call(
        pack_kernel,
        grid_spec=pltpu.PrefetchScalarGridSpec(
            num_scalar_prefetch=1,
            grid=(TOK // tile,),
            in_specs=[pl.BlockSpec((tile, D), lambda i, s: (i, 0))],
            out_specs=[pl.BlockSpec((tile, HALF), lambda i, s: (i, 0))] * 2,
        ),
        out_shape=[jax.ShapeDtypeStruct((TOK, HALF), BF)] * 2,
        compiler_params=params(40),
        cost_estimate=cost(0, 4 * TOK * D),
        name="pack",
    )(core, rows)


def turn_kernel(rows_ref, out_ref):
    out_ref[...] = rows_ref[...].T


def turn(rows):
    tile = 384
    return pl.pallas_call(
        turn_kernel,
        grid=(HALF // tile,),
        in_specs=[pl.BlockSpec((TOK, tile), lambda i: (0, i))],
        out_specs=pl.BlockSpec((tile, TOK), lambda i: (i, 0)),
        out_shape=jax.ShapeDtypeStruct((HALF, TOK), BF),
        compiler_params=params(40),
        cost_estimate=cost(0, 4 * TOK * HALF),
        name="turn",
    )(rows)


def dot(a, b):
    return jnp.dot(a, b, preferred_element_type=F32)


def project_first_kernel(at_ref, a0, a1, a2, w0, w1, w2, out_ref):
    out_ref[...] = dot(a0[...], w0[...]) + dot(a1[...], w1[...]) + dot(a2[...], w2[...])


def project_last_kernel(at_ref, a0, a1, a2, w0, w1, w2, acc_ref, wide_ref, out_ref):
    total = acc_ref[...] + (
        dot(a0[...], w0[...]) + dot(a1[...], w1[...]) + dot(a2[...], w2[...])
    )
    total = total * (1.0 / math.sqrt(D))
    wide_ref[...] = total
    out_ref[...] = total.astype(BF)


def project(at, rows, quads, acc=None):
    tile = 128

    def piece(part):
        return pl.BlockSpec((tile, QUAD), lambda i, s: (i, s[part]))

    whole = pl.BlockSpec((QUAD, KVW), lambda i, s: (0, 0))
    row = pl.BlockSpec((tile, KVW), lambda i, s: (i, 0))
    wide = jax.ShapeDtypeStruct((TOK, KVW), F32)
    first = acc is None
    return pl.pallas_call(
        project_first_kernel if first else project_last_kernel,
        grid_spec=pltpu.PrefetchScalarGridSpec(
            num_scalar_prefetch=1,
            grid=(TOK // tile,),
            in_specs=[piece(0), piece(1), piece(2), whole, whole, whole] + ([] if first else [row]),
            out_specs=row if first else [row, row],
        ),
        out_shape=wide if first else [wide, jax.ShapeDtypeStruct((TOK, KVW), BF)],
        compiler_params=params(40),
        cost_estimate=cost(2 * TOK * KVW * 3 * QUAD, 7 * MIB),
        name="project_first" if first else "project_last",
    )(at, rows, rows, rows, *quads, *([] if first else [acc]))


def grad_kernel(at_ref, a_ref, b_ref, ra_ref, rb_ref, out_ref):
    out_ref[...] = (dot(a_ref[...], ra_ref[...]) + dot(b_ref[...], rb_ref[...])).astype(
        out_ref.dtype
    )


def grad_block(at, turned, residuals, dtype):
    tile = 192
    steps = QUAD // tile
    piece = pl.BlockSpec((tile, TOK), lambda i, s: (s[0] * steps + i, 0))
    whole = pl.BlockSpec((TOK, KVW), lambda i, s: (0, 0))
    return pl.pallas_call(
        grad_kernel,
        grid_spec=pltpu.PrefetchScalarGridSpec(
            num_scalar_prefetch=1,
            grid=(steps,),
            in_specs=[piece, piece, whole, whole],
            out_specs=pl.BlockSpec((tile, KVW), lambda i, s: (i, 0)),
        ),
        out_shape=jax.ShapeDtypeStruct((QUAD, KVW), dtype),
        compiler_params=params(40),
        cost_estimate=cost(4 * QUAD * KVW * TOK, 4 * MIB),
        name="grad",
    )(at, *turned, *residuals)


def inner_kernel(grad_ref, w_ref, m_ref, v_ref, g_ref, m_out, v_out, w_out, delta_out):
    grad = grad_ref[...] * (1.0 / math.sqrt(TOK * 16))
    first = first_decay * m_ref[...] + (1.0 - first_decay) * grad
    second = second_decay * v_ref[...] + (1.0 - second_decay) * grad * grad
    m_out[...] = first
    v_out[...] = second
    wide = w_ref[...].astype(F32)
    weight = (
        wide - inner_rate * (first / (jnp.sqrt(second) + adam_eps) + weight_decay * wide)
    ).astype(BF)
    w_out[...] = weight
    delta = (g_ref[...] - weight.astype(F32)).astype(BF)
    for group in range(8):
        delta_out[group] = delta[:, 128 * group : 128 * group + 128]


def inner(grad, weight, first, second, base):
    row = pl.BlockSpec((PART, KVW), lambda i: (i, 0))
    wide = jax.ShapeDtypeStruct((UNIT, KVW), F32)
    return pl.pallas_call(
        inner_kernel,
        grid=(3,),
        in_specs=[row] * 5,
        out_specs=[row, row, row, pl.BlockSpec((8, PART, 128), lambda i: (0, i, 0))],
        out_shape=[
            wide,
            wide,
            jax.ShapeDtypeStruct((UNIT, KVW), BF),
            jax.ShapeDtypeStruct((8, UNIT, 128), BF),
        ],
        compiler_params=params(40),
        cost_estimate=cost(20 * UNIT * KVW, 9 * MIB),
        name="inner",
    )(grad, weight, first, second, base)


def total_kernel(parts_ref, out_ref):
    total = jnp.sum(parts_ref[...].astype(F32), axis=0)
    mean = (total * (1.0 / REPLICAS)).astype(BF)
    out_ref[...] = jnp.broadcast_to(mean[None], out_ref.shape)


def totals(parts):
    return pl.pallas_call(
        total_kernel,
        out_shape=jax.ShapeDtypeStruct(parts.shape, BF),
        compiler_params=params(40),
        cost_estimate=cost(0, 2 * MIB),
        name="totals",
    )(parts)


def outer_kernel(mean_ref, w_ref, g_ref, o_ref, local_out, global_out, momentum_out):
    mean = jnp.concatenate([mean_ref[group] for group in range(8)], axis=1).astype(F32)
    momentum = outer_mu * o_ref[...] + mean
    base = g_ref[...] - outer_rate * (mean + outer_mu * momentum)
    momentum_out[...] = momentum
    global_out[...] = base
    local_out[...] = (mix_keep * w_ref[...].astype(F32) + (1.0 - mix_keep) * base).astype(BF)


def outer(mean, weight, base, momentum):
    row = pl.BlockSpec((PART, KVW), lambda i: (i, 0))
    wide = jax.ShapeDtypeStruct((UNIT, KVW), F32)
    return pl.pallas_call(
        outer_kernel,
        grid=(3,),
        in_specs=[pl.BlockSpec((8, PART, 128), lambda i: (0, i, 0)), row, row, row],
        out_specs=[row, row, row],
        out_shape=[jax.ShapeDtypeStruct((UNIT, KVW), BF), wide, wide],
        compiler_params=params(40),
        cost_estimate=cost(8 * UNIT * KVW, 7 * MIB),
        name="outer",
    )(mean, weight, base, momentum)


def ordered(bit, own, other):
    size = own.shape[0]
    out = jnp.zeros((2 * size,) + own.shape[1:], own.dtype)
    out = lax.dynamic_update_slice(out, own, (bit * size, 0))
    return lax.dynamic_update_slice(out, other, ((1 - bit) * size, 0))


def half_at(value, index):
    size = value.shape[0] // 2
    return lax.dynamic_slice(value, (index * size, 0), (size, value.shape[1]))


def local(
    tokens, targets, local_weights, first_moment, second_moment, global_weights, outer_momentum
):
    rows = tokens[0]
    wanted = targets[0]
    weight = local_weights[0]
    bits, core = own_bits()
    core = core.astype(jnp.int32)
    quad_bits = [bits[ORDERS[part][2]] for part in range(3)]

    held = [weight[PART * part : PART * part + PART] for part in range(3)]
    for step in range(2):
        came = [flip(held[part], ORDERS[part][step]) for part in range(3)]
        held = [ordered(bits[ORDERS[part][step]], held[part], came[part]) for part in range(3)]
    far = [flip(held[part], ORDERS[part][2]) for part in range(3)]

    kept, sent = pack(core.reshape(1), rows)
    received = swap(sent)
    wanted_other = swap(wanted)
    near_at = jnp.stack([2 * part + quad_bits[part] for part in range(3)]).astype(jnp.int32)
    far_at = jnp.stack([2 * part + 1 - quad_bits[part] for part in range(3)]).astype(jnp.int32)
    turned = (turn(kept), turn(received))

    near_kept = project(near_at, kept, held)
    near_received = project(near_at, received, held)
    wide_kept, narrow_kept = project(far_at, kept, far, near_kept)
    cross_received = swap(narrow_kept)
    wide_received, narrow_received = project(far_at, received, far, near_received)
    cross_kept = swap(narrow_received)
    residuals = (
        (wide_kept + cross_kept.astype(F32) - wanted.astype(F32)).astype(BF),
        (wide_received + cross_received.astype(F32) - wanted_other.astype(F32)).astype(BF),
    )

    came = []
    for part in range(3):
        away = grad_block(far_at[part : part + 1], turned, residuals, BF)
        came.append(flip(away, ORDERS[part][2]))
    sums = []
    for part in range(3):
        stay = grad_block(near_at[part : part + 1], turned, residuals, F32)
        sums.append(stay + came[part].astype(F32))
    for step in (1, 0):
        away = []
        for part in range(3):
            bit = bits[ORDERS[part][step]]
            away.append(flip(half_at(sums[part], 1 - bit).astype(BF), ORDERS[part][step]))
        for part in range(3):
            bit = bits[ORDERS[part][step]]
            sums[part] = half_at(sums[part], bit) + away[part].astype(F32)
    grad = jnp.concatenate(sums, axis=0)

    first, second, weight, delta = inner(
        grad, weight, first_moment[0], second_moment[0], global_weights
    )
    pieces = lax.all_to_all(delta.reshape(REPLICAS, UNIT // 2, 128), "replica", 0, 0)
    mean = lax.all_to_all(totals(pieces), "replica", 0, 0).reshape(8, UNIT, 128)
    new_local, new_global, new_momentum = outer(mean, weight, global_weights, outer_momentum)
    return (new_local[None], first[None], second[None], new_global, new_momentum)


def solution(mesh):
    return jax.shard_map(
        local,
        mesh=mesh,
        in_specs=(
            P("replica", "fsdp", None),
            P("replica", "fsdp", None),
            P("replica", "fsdp", None),
            P("replica", "fsdp", None),
            P("replica", "fsdp", None),
            P("fsdp", None),
            P("fsdp", None),
        ),
        out_specs=(
            P("replica", "fsdp", None),
            P("replica", "fsdp", None),
            P("replica", "fsdp", None),
            P("fsdp", None),
            P("fsdp", None),
        ),
        check_vma=False,
    )
```

time: 402 us -> 176 us (0.44)
  waiting for transfers between devices: 324 us -> 36.4 us
  blocking collectives: 0 us -> 46.6 us
  Pallas kernels: 0 us -> 39.7 us
  starting transfers between devices: 0.12 us -> 27.9 us
  matrix products: 19 us -> 0 us
  local copies, waits for them, and re-layouts: 34.8 us -> 18.9 us
  between operations: 13.8 us -> 1.08 us
  other arithmetic: 9.3 us -> 4.97 us
    psum x1 -> x0, waiting for transfers between devices: 130 us -> none  [local(): lax.psum(delta.astype(jnp.float32).astype(jnp.bfloat16), 'replica')]
    unnamed x4 -> x0, waiting for transfers between devices: 108 us -> none
    all_gather x1 -> x0, waiting for transfers between devices: 86.7 us -> none  [local(): lax.all_gather(weight, 'fsdp', axis=0, tiled=True)]
    all_to_all x0 -> x2, blocking collectives: none -> 46.6 us  [the longest x1 26.7 us: local(): lax.all_to_all(delta.reshape(REPLICAS, UNIT // 2, 128), 'replica', 0, 0)]
    pallas_call x0 -> x16, Pallas kernels: none -> 39.7 us  [the longest x4 19.5 us: project(): pl.pallas_call(project_first_kernel if first else project_last_kernel, gr...]
    ppermute x0 -> x22, waiting for transfers between devices: none -> 36.4 us  [the longest x18 36.4 us: flip(): return lax.ppermute(value, 'fsdp', [(i, i ^ FLIP[dim]) for i in range(16)])]
    unnamed x20 -> x14, local copies, waits for them, and re-layouts: 34.8 us -> 2.37 us
    ppermute x0 -> x22, starting transfers between devices: none -> 27.9 us  [the longest x18 26.9 us: flip(): return lax.ppermute(value, 'fsdp', [(i, i ^ FLIP[dim]) for i in range(16)])]
  transfers between devices with their start and end apart: 3 -> 22, of which waited for: 3 -> 10; matrix products, arithmetic and copies ran while one was open for 3% -> 10% of each run, Pallas kernels for 0% -> 19%
where the time goes in v1:
time: 176 us; the launch traced here: 175 us
  blocking collectives  46.6 us (26%)
  Pallas kernels  39.7 us (23%)
  waiting for transfers between devices  36.4 us (21%)
  starting transfers between devices  27.9 us (16%)
  local copies, waits for them, and re-layouts  18.9 us (11%)
  other arithmetic  4.97 us (3%)
    ppermute x18, waiting for transfers between devices, flip(): return lax.ppermute(value, 'fsdp', [(i, i ^ FLIP[dim]) for i in range(16)])  36.4 us
    ppermute x18, starting transfers between devices, flip(): return lax.ppermute(value, 'fsdp', [(i, i ^ FLIP[dim]) for i in range(16)])  26.9 us
    all_to_all x1, blocking collectives, local(): lax.all_to_all(delta.reshape(REPLICAS, UNIT // 2, 128), 'replica', 0, 0)  26.7 us
    all_to_all x1, blocking collectives, local(): mean = lax.all_to_all(totals(pieces), 'replica', 0, 0).reshape(8, UNIT, 128)  19.8 us
    pallas_call x4, Pallas kernels, project(): pl.pallas_call(project_first_kernel if first else project_last_kernel, gr...  19.5 us
    pallas_call x6, Pallas kernels, grad_block(): pl.pallas_call(grad_kernel, grid_spec=pltpu.PrefetchScalarGridSpec(num_sc...  7.4 us
    dynamic_update_slice x6, local copies, waits for them, and re-layouts, ordered(): return lax.dynamic_update_slice(out, other, ((1 - bit) * size, 0))  5.76 us
    dynamic_update_slice x6, local copies, waits for them, and re-layouts, ordered(): out = lax.dynamic_update_slice(out, own, (bit * size, 0))  4.97 us
  transfers between devices with their start and end apart: 22, of which 10 were waited for; matrix products, arithmetic and copies ran while one was open for 10% of the time, Pallas kernels for 19%

profile of v1, /device:TPU:2, one launch (start us, length us, event | category | flops | bytes accessed | tf_op | source)
XLA Modules:
  0.0 175.5 jit_solution(18428470604882738159)
XLA Ops:
  0.6 1.9 %slice_bitcast_fusion = (bf16[96,1024]{1,0:T(8,128)(2,1)}, bf16[96,1024]{1,0:T(8,128)(2,1)S(1)}, bf16[96,1024]{1,0:T(8,128)(2,1)}) fusion(bf16[1,288,1024]{2,1,0:T(8,128)(2,1)} %param.9), kind=kLoop, calls=%fused_computation.18 | loop fusion | bytes 1179648 | tf_op jit(solution)/shard_map/slice | solution.py:302
  2.5 2.3 %collective-permute-start.1 = (bf16[96,1024]{1,0:T(8,128)(2,1)}, bf16[96,1024]{1,0:T(8,128)(2,1)}, u32[]{:S(2)}, u32[]{:S(2)}) collective-permute-start(bf16[96,1024]{1,0:T(8,128)(2,1)} %get-tuple-element.33), channel_id=1, source_target_pairs={{0,2},{1,3},{2,0},{3,1},{4,6},{5,7},{6,4},{7,5},{8,10},{9,11},{10,... | collective-permute-start | bytes 589832 | tf_op jit(solution)/shard_map/ppermute | solution.py:61
  6.3 2.2 %collective-permute-start.4 = (bf16[96,1024]{1,0:T(8,128)(2,1)S(1)}, bf16[96,1024]{1,0:T(8,128)(2,1)}, u32[]{:S(2)}, u32[]{:S(2)}) collective-permute-start(bf16[96,1024]{1,0:T(8,128)(2,1)S(1)} %get-tuple-element.32), channel_id=1, source_target_pairs={{0,6},{1,7},{2,4},{3,5},{4,2},{5,3},{6,0},{7,1},{8,14},{9,15},{10,... | collective-permute-start | bytes 589832 | tf_op jit(solution)/shard_map/ppermute | solution.py:61
  8.4 2.3 %copy-done.2 = bf16[1,512,4608]{2,1,0:T(8,128)(2,1)S(1)} copy-done((bf16[1,512,4608]{2,1,0:T(8,128)(2,1)S(1)}, bf16[1,512,4608]{2,1,0:T(8,128)(2,1)}, u32[]{:S(2)}) %copy-start.2) | copy-done | bytes 4718616
  10.8 3.2 %pack.1 = (bf16[512,2304]{1,0:T(8,128)(2,1)S(1)}, bf16[512,2304]{1,0:T(8,128)(2,1)}) custom-call(s32[1]{0:T(128)} %bitcast.1.core_ref, bf16[512,4608]{1,0:T(8,128)(2,1)S(1)} %bitcast.31), custom_call_target="tpu_custom_call" | custom-call | bytes 9437184 | tf_op jit(solution)/shard_map/pack/pallas_call | solution.py:103
  19.7 2.5 %collective-permute-start.8 = (bf16[192,1024]{1,0:T(8,128)(2,1)}, bf16[192,1024]{1,0:T(8,128)(2,1)S(1)}, u32[]{:S(2)}, u32[]{:S(2)}) collective-permute-start(bf16[192,1024]{1,0:T(8,128)(2,1)} %constant_dynamic-update-slice_fusion.2), channel_id=1, source_target_pairs={{0,2},{1,3},{2,0},{3,1},{4,6},{5,7},{6,4},{7,5},{8,10},{9,11},{10,... | collective-permute-start | bytes 1179656 | tf_op jit(solution)/shard_map/ppermute | solution.py:61
  30.8 2.9 %collective-permute-start.3 = (bf16[384,1024]{1,0:T(8,128)(2,1)}, bf16[384,1024]{1,0:T(8,128)(2,1)}, u32[]{:S(2)}, u32[]{:S(2)}) collective-permute-start(bf16[384,1024]{1,0:T(8,128)(2,1)} %constant_dynamic-update-slice_fusion.8.w0), channel_id=1, source_target_pairs={{0,8},{1,9},{2,10},{3,11},{4,12},{5,13},{6,14},{7,15},{8,0},{9,1},... | collective-permute-start | bytes 2359304 | tf_op jit(solution)/shard_map/ppermute | solution.py:61
  37.9 4.5 %project_first.2.acc_ref = f32[512,1024]{1,0:T(8,128)S(1)} custom-call(s32[3]{0:T(128)S(1)} %get-tuple-element.35.at_ref, bf16[512,2304]{1,0:T(8,128)(2,1)S(1)} %get-tuple-element.18.rows_ref.a0.a1.a2, bf16[512,2304]{1,0:T(8,128)(2,1)S(1)} %get-tuple-element.18.rows_ref.a0.a1.a2, bf16[512,2304]{1,0:T(8,128)(2,1)S(1)} %get-tuple-element.18.rows_ref.a0.a1.a2, ...), custom_call_target="tpu_custom_call" | custom-call | flops 1207959552 | bytes 7340032 | tf_op jit(solution)/shard_map/project_first/pallas_call | solution.py:163
  42.4 11.1 %collective-permute-done.3.w0 = bf16[384,1024]{1,0:T(8,128)(2,1)} collective-permute-done((bf16[384,1024]{1,0:T(8,128)(2,1)}, bf16[384,1024]{1,0:T(8,128)(2,1)}, u32[]{:S(2)}, u32[]{:S(2)}) %collective-permute-start.3) | collective-permute-done | bytes 786464 | tf_op jit(solution)/shard_map/ppermute | solution.py:61
  55.3 4.8 %project_last.2 = (f32[512,1024]{1,0:T(8,128)S(1)}, bf16[512,1024]{1,0:T(8,128)(2,1)S(1)}) custom-call(s32[3]{0:T(128)S(1)} %get-tuple-element.34.at_ref, bf16[512,2304]{1,0:T(8,128)(2,1)S(1)} %get-tuple-element.18.rows_ref.a0.a1.a2, bf16[512,2304]{1,0:T(8,128)(2,1)S(1)} %get-tuple-element.18.rows_ref.a0.a1.a2, ...), custom_call_target="tpu_custom_call" | custom-call | flops 1207959552 | bytes 7340032 | tf_op jit(solution)/shard_map/project_last/pallas_call | solution.py:163
  60.2 5.0 %project_first.3.acc_ref = f32[512,1024]{1,0:T(8,128)S(1)} custom-call(s32[3]{0:T(128)S(1)} %get-tuple-element.35.at_ref, bf16[512,2304]{1,0:T(8,128)(2,1)} %collective-permute-done.rows_ref.a0.a1.a2, bf16[512,2304]{1,0:T(8,128)(2,1)} %collective-permute-done.rows_ref.a0.a1.a2, bf16[512,2304]{1,0:T(8,128)(2,1)} %collective-permute-done.rows_ref.a0.a1.a2, ...), custom_call_target="tpu_custom_call" | custom-call | flops 1207959552 | bytes 7340032 | tf_op jit(solution)/shard_map/project_first/pallas_call | solution.py:163
  65.2 5.3 %project_last.3 = (f32[512,1024]{1,0:T(8,128)S(1)}, bf16[512,1024]{1,0:T(8,128)(2,1)S(1)}) custom-call(s32[3]{0:T(128)S(1)} %get-tuple-element.34.at_ref, bf16[512,2304]{1,0:T(8,128)(2,1)} %collective-permute-done.rows_ref.a0.a1.a2, bf16[512,2304]{1,0:T(8,128)(2,1)} %collective-permute-done.rows_ref.a0.a1.a2, ...), custom_call_target="tpu_custom_call" | custom-call | flops 1207959552 | bytes 7340032 | tf_op jit(solution)/shard_map/project_last/pallas_call | solution.py:163
  72.5 3.7 %turn.3.b_ref = bf16[2304,512]{1,0:T(8,128)(2,1)S(1)} custom-call(bf16[512,2304]{1,0:T(8,128)(2,1)} %collective-permute-done.rows_ref.a0.a1.a2), custom_call_target="tpu_custom_call" | custom-call | bytes 4718592 | tf_op jit(solution)/shard_map/turn/pallas_call | solution.py:124
  76.2 1.8 %subtract_convert_fusion.rb_ref = bf16[512,1024]{1,0:T(8,128)(2,1)S(1)} fusion(bf16[512,1024]{1,0:T(8,128)(2,1)} %collective-permute-done.12, f32[512,1024]{1,0:T(8,128)S(1)} %get-tuple-element.22, bf16[512,1024]{1,0:T(8,128)(2,1)S(1)} %collective-permute-done.11), kind=kLoop, calls=%fused_computation | loop fusion | flops 2621440 | bytes 5242880 | tf_op jit(solution)/shard_map/convert_element_type | solution.py:323
  78.0 1.8 %subtract_convert_fusion.1.ra_ref = bf16[512,1024]{1,0:T(8,128)(2,1)S(1)} fusion(f32[512,1024]{1,0:T(8,128)S(1)} %get-tuple-element.20, bf16[512,1024]{1,0:T(8,128)(2,1)S(1)} %collective-permute-done.10, bf16[1,512,1024]{2,1,0:T(8,128)(2,1)} %param.8), kind=kLoop, calls=%fused_computation.1 | loop fusion | flops 2621440 | bytes 5242880 | tf_op jit(solution)/shard_map/convert_element_type | solution.py:322
  82.9 1.9 %collective-permute-start.16 = (bf16[384,1024]{1,0:T(8,128)(2,1)S(1)}, bf16[384,1024]{1,0:T(8,128)(2,1)S(1)}, u32[]{:S(2)}, u32[]{:S(2)}) collective-permute-start(bf16[384,1024]{1,0:T(8,128)(2,1)S(1)} %grad.9), channel_id=1, source_target_pairs={{0,2},{1,3},{2,0},{3,1},{4,6},{5,7},{6,4},{7,5},{8,10},{9,11},{10,... | collective-permute-start | bytes 2359304 | tf_op jit(solution)/shard_map/ppermute | solution.py:61
  90.9 11.2 %collective-permute-done.13 = bf16[384,1024]{1,0:T(8,128)(2,1)S(1)} collective-permute-done((bf16[384,1024]{1,0:T(8,128)(2,1)S(1)}, bf16[384,1024]{1,0:T(8,128)(2,1)S(1)}, u32[]{:S(2)}, u32[]{:S(2)}) %collective-permute-start.13) | collective-permute-done | bytes 786464 | tf_op jit(solution)/shard_map/ppermute | solution.py:61
  107.5 6.1 %collective-permute-done.14 = bf16[192,1024]{1,0:T(8,128)(2,1)S(1)} collective-permute-done((bf16[192,1024]{1,0:T(8,128)(2,1)S(1)}, bf16[192,1024]{1,0:T(8,128)(2,1)S(1)}, u32[]{:S(2)}, u32[]{:S(2)}) %collective-permute-start.14) | collective-permute-done | bytes 393248 | tf_op jit(solution)/shard_map/ppermute | solution.py:61
  116.8 3.3 %collective-permute-start.21 = (bf16[96,1024]{1,0:T(8,128)(2,1)S(1)}, bf16[96,1024]{1,0:T(8,128)(2,1)S(1)}, u32[]{:S(2)}, u32[]{:S(2)}) collective-permute-start(bf16[96,1024]{1,0:T(8,128)(2,1)S(1)} %dynamic-slice_convert_fusion.3), channel_id=1, source_target_pairs={{0,8},{1,9},{2,10},{3,11},{4,12},{5,13},{6,14},{7,15},{8,0},{9,1},... | collective-permute-start | bytes 589832 | tf_op jit(solution)/shard_map/ppermute | solution.py:61
  121.9 2.2 %collective-permute-done.21 = bf16[96,1024]{1,0:T(8,128)(2,1)S(1)} collective-permute-done((bf16[96,1024]{1,0:T(8,128)(2,1)S(1)}, bf16[96,1024]{1,0:T(8,128)(2,1)S(1)}, u32[]{:S(2)}, u32[]{:S(2)}) %collective-permute-start.21) | collective-permute-done | bytes 196640 | tf_op jit(solution)/shard_map/ppermute | solution.py:61
  124.3 2.4 %inner.1 = (f32[288,1024]{1,0:T(8,128)}, f32[288,1024]{1,0:T(8,128)}, bf16[288,1024]{1,0:T(8,128)(2,1)S(1)}, bf16[8,288,128]{2,1,0:T(8,128)(2,1)S(1)}) custom-call(f32[288,1024]{1,0:T(8,128)S(1)} %pad_maximum_fusion.grad_ref, bf16[288,1024]{1,0:T(8,128)(2,1)S(1)} %bitcast.30, f32[288,1024]{1,0:T(8,128)S(1)} %bitcast.33, f32[288,1024]{1,0:T(8,128)S(1)} %bitcast.34, ...), custom_call_target="tpu_custom_call" | custom-call | flops 5898240 | bytes 9437184 | tf_op jit(solution)/shard_map/inner/pallas_call | solution.py:223
  126.7 26.7 %all_to_all.10.parts_ref = bf16[16,144,128]{2,1,0:T(8,128)(2,1)S(1)} all-to-all(bf16[16,144,128]{2,1,0:T(8,128)(2,1)S(1)} %bitcast.35), channel_id=1, replica_groups=mesh['replica'=16,'fsdp'=16] {'replica'}, dimensions={0} | all-to-all | bytes 1179648 | tf_op jit(solution)/shard_map/all_to_all | solution.py:347
  153.5 19.8 %all_to_all.11 = bf16[16,144,128]{2,1,0:T(8,128)(2,1)S(1)} all-to-all(bf16[16,144,128]{2,1,0:T(8,128)(2,1)S(1)} %totals.1), channel_id=1, replica_groups=mesh['replica'=16,'fsdp'=16] {'replica'}, dimensions={0} | all-to-all | bytes 1179648 | tf_op jit(solution)/shard_map/all_to_all | solution.py:348
  173.4 2.1 %outer.1 = (bf16[288,1024]{1,0:T(8,128)(2,1)}, f32[288,1024]{1,0:T(8,128)}, f32[288,1024]{1,0:T(8,128)}) custom-call(bf16[8,288,128]{2,1,0:T(8,128)(2,1)S(1)} %bitcast.32, bf16[288,1024]{1,0:T(8,128)(2,1)S(1)} %get-tuple-element.25.w_ref, f32[288,1024]{1,0:T(8,128)S(1)} %copy-done.3, f32[288,1024]{1,0:T(8,128)S(1)} %copy-done.4), custom_call_target="tpu_custom_call" | custom-call | flops 2359296 | bytes 7340032 | tf_op jit(solution)/shard_map/outer/pallas_call | solution.py:268
  (90 shorter events, 43.3 us)
Async XLA Ops:
  2.5 14.5 %collective-permute-start.1 = (bf16[96,1024]{1,0:T(8,128)(2,1)}, bf16[96,1024]{1,0:T(8,128)(2,1)}, u32[]{:S(2)}, u32[]{:S(2)}) collective-permute-start(bf16[96,1024]{1,0:T(8,128)(2,1)} %get-tuple-element.33), channel_id=1, source_target_pairs={{0,2},{1,3},{2,0},{3,1},{4,6},{5,7},{6,4},{7,5},{8,10},{9,11},{10,... | collective-permute-start | bytes 589832 | tf_op jit(solution)/shard_map/ppermute | solution.py:61
  4.8 13.3 %collective-permute-start.7 = (bf16[96,1024]{1,0:T(8,128)(2,1)}, bf16[96,1024]{1,0:T(8,128)(2,1)}, u32[]{:S(2)}, u32[]{:S(2)}) collective-permute-start(bf16[96,1024]{1,0:T(8,128)(2,1)} %get-tuple-element.31), channel_id=1, source_target_pairs={{0,8},{1,9},{2,10},{3,11},{4,12},{5,13},{6,14},{7,15},{8,0},{9,1},... | collective-permute-start | bytes 589832 | tf_op jit(solution)/shard_map/ppermute | solution.py:61
  6.3 16.0 %collective-permute-start.4 = (bf16[96,1024]{1,0:T(8,128)(2,1)S(1)}, bf16[96,1024]{1,0:T(8,128)(2,1)}, u32[]{:S(2)}, u32[]{:S(2)}) collective-permute-start(bf16[96,1024]{1,0:T(8,128)(2,1)S(1)} %get-tuple-element.32), channel_id=1, source_target_pairs={{0,6},{1,7},{2,4},{3,5},{4,2},{5,3},{6,0},{7,1},{8,14},{9,15},{10,... | collective-permute-start | bytes 589832 | tf_op jit(solution)/shard_map/ppermute | solution.py:61
  10.8 3.3 %copy-start = (bf16[1,288,1024]{2,1,0:T(8,128)(2,1)S(1)}, bf16[1,288,1024]{2,1,0:T(8,128)(2,1)}, u32[]{:S(2)}) copy-start(bf16[1,288,1024]{2,1,0:T(8,128)(2,1)} %param.9) | copy-start | bytes 1769476
  14.0 46.2 %collective-permute-start = (bf16[512,2304]{1,0:T(8,128)(2,1)}, bf16[512,2304]{1,0:T(8,128)(2,1)}, u32[]{:S(2)}, u32[]{:S(2)}) collective-permute-start(bf16[512,2304]{1,0:T(8,128)(2,1)} %get-tuple-element.19), channel_id=1, source_target_pairs={{0,1},{1,0},{2,3},{3,2},{4,5},{5,4},{6,7},{7,6},{8,9},{9,8},{10,11... | collective-permute-start | bytes 7077896 | tf_op jit(solution)/shard_map/ppermute | solution.py:65
  18.0 12.1 %collective-permute-start.2 = (bf16[192,1024]{1,0:T(8,128)(2,1)S(1)}, bf16[192,1024]{1,0:T(8,128)(2,1)S(1)}, u32[]{:S(2)}, u32[]{:S(2)}) collective-permute-start(bf16[192,1024]{1,0:T(8,128)(2,1)S(1)} %constant_dynamic-update-slice_fusion.10), channel_id=1, source_target_pairs={{0,6},{1,7},{2,4},{3,5},{4,2},{5,3},{6,0},{7,1},{8,14},{9,15},{10,... | collective-permute-start | bytes 1179656 | tf_op jit(solution)/shard_map/ppermute | solution.py:61
  19.7 14.1 %collective-permute-start.8 = (bf16[192,1024]{1,0:T(8,128)(2,1)}, bf16[192,1024]{1,0:T(8,128)(2,1)S(1)}, u32[]{:S(2)}, u32[]{:S(2)}) collective-permute-start(bf16[192,1024]{1,0:T(8,128)(2,1)} %constant_dynamic-update-slice_fusion.2), channel_id=1, source_target_pairs={{0,2},{1,3},{2,0},{3,1},{4,6},{5,7},{6,4},{7,5},{8,10},{9,11},{10,... | collective-permute-start | bytes 1179656 | tf_op jit(solution)/shard_map/ppermute | solution.py:61
  23.9 13.7 %collective-permute-start.5 = (bf16[192,1024]{1,0:T(8,128)(2,1)}, bf16[192,1024]{1,0:T(8,128)(2,1)S(1)}, u32[]{:S(2)}, u32[]{:S(2)}) collective-permute-start(bf16[192,1024]{1,0:T(8,128)(2,1)} %constant_dynamic-update-slice_fusion.6), channel_id=1, source_target_pairs={{0,8},{1,9},{2,10},{3,11},{4,12},{5,13},{6,14},{7,15},{8,0},{9,1},... | collective-permute-start | bytes 1179656 | tf_op jit(solution)/shard_map/ppermute | solution.py:61
  30.8 22.7 %collective-permute-start.3 = (bf16[384,1024]{1,0:T(8,128)(2,1)}, bf16[384,1024]{1,0:T(8,128)(2,1)}, u32[]{:S(2)}, u32[]{:S(2)}) collective-permute-start(bf16[384,1024]{1,0:T(8,128)(2,1)} %constant_dynamic-update-slice_fusion.8.w0), channel_id=1, source_target_pairs={{0,8},{1,9},{2,10},{3,11},{4,12},{5,13},{6,14},{7,15},{8,0},{9,1},... | collective-permute-start | bytes 2359304 | tf_op jit(solution)/shard_map/ppermute | solution.py:61
  34.6 19.1 %collective-permute-start.9 = (bf16[384,1024]{1,0:T(8,128)(2,1)}, bf16[384,1024]{1,0:T(8,128)(2,1)}, u32[]{:S(2)}, u32[]{:S(2)}) collective-permute-start(bf16[384,1024]{1,0:T(8,128)(2,1)} %constant_dynamic-update-slice_fusion.w2), channel_id=1, source_target_pairs={{0,6},{1,7},{2,4},{3,5},{4,2},{5,3},{6,0},{7,1},{8,14},{9,15},{10,... | collective-permute-start | bytes 2359304 | tf_op jit(solution)/shard_map/ppermute | solution.py:61
  37.6 17.7 %collective-permute-start.6 = (bf16[384,1024]{1,0:T(8,128)(2,1)S(1)}, bf16[384,1024]{1,0:T(8,128)(2,1)}, u32[]{:S(2)}, u32[]{:S(2)}) collective-permute-start(bf16[384,1024]{1,0:T(8,128)(2,1)S(1)} %constant_dynamic-update-slice_fusion.4.w1), channel_id=1, source_target_pairs={{0,2},{1,3},{2,0},{3,1},{4,6},{5,7},{6,4},{7,5},{8,10},{9,11},{10,... | collective-permute-start | bytes 2359304 | tf_op jit(solution)/shard_map/ppermute | solution.py:61
  37.7 38.5 %collective-permute-start.12 = (bf16[512,1024]{1,0:T(8,128)(2,1)}, bf16[512,1024]{1,0:T(8,128)(2,1)}, u32[]{:S(2)}, u32[]{:S(2)}) collective-permute-start(bf16[512,1024]{1,0:T(8,128)(2,1)} %bitcast.11), channel_id=1, source_target_pairs={{0,1},{1,0},{2,3},{3,2},{4,5},{5,4},{6,7},{7,6},{8,9},{9,8},{10,11... | collective-permute-start | bytes 3145736 | tf_op jit(solution)/shard_map/ppermute | solution.py:65
  60.1 16.1 %collective-permute-start.11 = (bf16[512,1024]{1,0:T(8,128)(2,1)S(1)}, bf16[512,1024]{1,0:T(8,128)(2,1)S(1)}, u32[]{:S(2)}, u32[]{:S(2)}) collective-permute-start(bf16[512,1024]{1,0:T(8,128)(2,1)S(1)} %get-tuple-element.23), channel_id=1, source_target_pairs={{0,1},{1,0},{2,3},{3,2},{4,5},{5,4},{6,7},{7,6},{8,9},{9,8},{10,11... | collective-permute-start | bytes 3145736 | tf_op jit(solution)/shard_map/ppermute | solution.py:65
  70.5 7.5 %collective-permute-start.10 = (bf16[512,1024]{1,0:T(8,128)(2,1)S(1)}, bf16[512,1024]{1,0:T(8,128)(2,1)S(1)}, u32[]{:S(2)}, u32[]{:S(2)}) collective-permute-start(bf16[512,1024]{1,0:T(8,128)(2,1)S(1)} %get-tuple-element.21), channel_id=1, source_target_pairs={{0,1},{1,0},{2,3},{3,2},{4,5},{5,4},{6,7},{7,6},{8,9},{9,8},{10,11... | collective-permute-start | bytes 3145736 | tf_op jit(solution)/shard_map/ppermute | solution.py:65
  81.0 21.1 %collective-permute-start.13 = (bf16[384,1024]{1,0:T(8,128)(2,1)S(1)}, bf16[384,1024]{1,0:T(8,128)(2,1)S(1)}, u32[]{:S(2)}, u32[]{:S(2)}) collective-permute-start(bf16[384,1024]{1,0:T(8,128)(2,1)S(1)} %grad.7), channel_id=1, source_target_pairs={{0,8},{1,9},{2,10},{3,11},{4,12},{5,13},{6,14},{7,15},{8,0},{9,1},... | collective-permute-start | bytes 2359304 | tf_op jit(solution)/shard_map/ppermute | solution.py:61
  82.9 21.1 %collective-permute-start.16 = (bf16[384,1024]{1,0:T(8,128)(2,1)S(1)}, bf16[384,1024]{1,0:T(8,128)(2,1)S(1)}, u32[]{:S(2)}, u32[]{:S(2)}) collective-permute-start(bf16[384,1024]{1,0:T(8,128)(2,1)S(1)} %grad.9), channel_id=1, source_target_pairs={{0,2},{1,3},{2,0},{3,1},{4,6},{5,7},{6,4},{7,5},{8,10},{9,11},{10,... | collective-permute-start | bytes 2359304 | tf_op jit(solution)/shard_map/ppermute | solution.py:61
  86.1 19.7 %collective-permute-start.19 = (bf16[384,1024]{1,0:T(8,128)(2,1)S(1)}, bf16[384,1024]{1,0:T(8,128)(2,1)S(1)}, u32[]{:S(2)}, u32[]{:S(2)}) collective-permute-start(bf16[384,1024]{1,0:T(8,128)(2,1)S(1)} %grad.11), channel_id=1, source_target_pairs={{0,6},{1,7},{2,4},{3,5},{4,2},{5,3},{6,0},{7,1},{8,14},{9,15},{10,... | collective-permute-start | bytes 2359304 | tf_op jit(solution)/shard_map/ppermute | solution.py:61
  102.5 11.1 %collective-permute-start.14 = (bf16[192,1024]{1,0:T(8,128)(2,1)S(1)}, bf16[192,1024]{1,0:T(8,128)(2,1)S(1)}, u32[]{:S(2)}, u32[]{:S(2)}) collective-permute-start(bf16[192,1024]{1,0:T(8,128)(2,1)S(1)} %dynamic-slice_convert_fusion.2), channel_id=1, source_target_pairs={{0,6},{1,7},{2,4},{3,5},{4,2},{5,3},{6,0},{7,1},{8,14},{9,15},{10,... | collective-permute-start | bytes 1179656 | tf_op jit(solution)/shard_map/ppermute | solution.py:61
  104.4 11.5 %collective-permute-start.17 = (bf16[192,1024]{1,0:T(8,128)(2,1)S(1)}, bf16[192,1024]{1,0:T(8,128)(2,1)S(1)}, u32[]{:S(2)}, u32[]{:S(2)}) collective-permute-start(bf16[192,1024]{1,0:T(8,128)(2,1)S(1)} %dynamic-slice_convert_fusion.1), channel_id=1, source_target_pairs={{0,8},{1,9},{2,10},{3,11},{4,12},{5,13},{6,14},{7,15},{8,0},{9,1},... | collective-permute-start | bytes 1179656 | tf_op jit(solution)/shard_map/ppermute | solution.py:61
  106.1 10.5 %collective-permute-start.20 = (bf16[192,1024]{1,0:T(8,128)(2,1)S(1)}, bf16[192,1024]{1,0:T(8,128)(2,1)S(1)}, u32[]{:S(2)}, u32[]{:S(2)}) collective-permute-start(bf16[192,1024]{1,0:T(8,128)(2,1)S(1)} %dynamic-slice_convert_fusion), channel_id=1, source_target_pairs={{0,2},{1,3},{2,0},{3,1},{4,6},{5,7},{6,4},{7,5},{8,10},{9,11},{10,... | collective-permute-start | bytes 1179656 | tf_op jit(solution)/shard_map/ppermute | solution.py:61
  113.7 6.4 %collective-permute-start.15 = (bf16[96,1024]{1,0:T(8,128)(2,1)S(1)}, bf16[96,1024]{1,0:T(8,128)(2,1)S(1)}, u32[]{:S(2)}, u32[]{:S(2)}) collective-permute-start(bf16[96,1024]{1,0:T(8,128)(2,1)S(1)} %dynamic-slice_convert_fusion.5), channel_id=1, source_target_pairs={{0,2},{1,3},{2,0},{3,1},{4,6},{5,7},{6,4},{7,5},{8,10},{9,11},{10,... | collective-permute-start | bytes 589832 | tf_op jit(solution)/shard_map/ppermute | solution.py:61
  116.0 5.8 %collective-permute-start.18 = (bf16[96,1024]{1,0:T(8,128)(2,1)S(1)}, bf16[96,1024]{1,0:T(8,128)(2,1)S(1)}, u32[]{:S(2)}, u32[]{:S(2)}) collective-permute-start(bf16[96,1024]{1,0:T(8,128)(2,1)S(1)} %dynamic-slice_convert_fusion.4), channel_id=1, source_target_pairs={{0,6},{1,7},{2,4},{3,5},{4,2},{5,3},{6,0},{7,1},{8,14},{9,15},{10,... | collective-permute-start | bytes 589832 | tf_op jit(solution)/shard_map/ppermute | solution.py:61
  116.8 7.3 %collective-permute-start.21 = (bf16[96,1024]{1,0:T(8,128)(2,1)S(1)}, bf16[96,1024]{1,0:T(8,128)(2,1)S(1)}, u32[]{:S(2)}, u32[]{:S(2)}) collective-permute-start(bf16[96,1024]{1,0:T(8,128)(2,1)S(1)} %dynamic-slice_convert_fusion.3), channel_id=1, source_target_pairs={{0,8},{1,9},{2,10},{3,11},{4,12},{5,13},{6,14},{7,15},{8,0},{9,1},... | collective-permute-start | bytes 589832 | tf_op jit(solution)/shard_map/ppermute | solution.py:61
  126.7 46.7 %copy-start.4 = (f32[288,1024]{1,0:T(8,128)S(1)}, f32[288,1024]{1,0:T(8,128)}, u32[]{:S(2)}) copy-start(f32[288,1024]{1,0:T(8,128)} %o_ref.1) | copy-start | bytes 3538948
  (5 other events, 12.1 us)

commit v2 on v1

v2 whole, which is shorter than its diff:
```python
import math

import jax
import jax.numpy as jnp
from jax import lax
from jax.experimental import pallas as pl
from jax.experimental.pallas import tpu as pltpu
from jax.sharding import PartitionSpec as P

inner_rate = 0.02
first_decay = 0.5
second_decay = 0.95
adam_eps = 1e-08
weight_decay = 0.1
outer_rate = 0.7
outer_mu = 0.9
mix_keep = 0.5

BF = jnp.bfloat16
F32 = jnp.float32

D = 4608
KVW = 1024
TOK = 512
UNIT = 288
HALF = 2304
REPLICAS = 16
MIB = 1024 * 1024

EVEN, ODD, WIDE = 0, 1, 2
PART = 96
QUAD = 4 * PART
PARTS = range(3)
ORDERS = ((EVEN, ODD, WIDE), (ODD, WIDE, EVEN), (WIDE, EVEN, ODD))
FLIP = {EVEN: 2, ODD: 6, WIDE: 8}
SWAP_LAST = [(i, i ^ 1) for i in range(16)]
ALONG_Z = [list(range(0, 16, 2)), list(range(1, 16, 2))]


def chip_bit(chip, dim):
    x = chip % 4
    if dim == EVEN:
        return (x ^ (x // 2)) % 2
    if dim == ODD:
        return x // 2
    return chip // 4


def unit_order(part):
    one, two, three = ORDERS[part]
    return sorted(
        range(8), key=lambda chip: (chip_bit(chip, three), chip_bit(chip, two), chip_bit(chip, one))
    )


def own_bits():
    me = lax.axis_index("fsdp")
    core = me & 1
    x = (me >> 1) & 3
    bits = {EVEN: (x ^ (x >> 1)) & 1, ODD: x >> 1, WIDE: me >> 3}
    places = [[bits[dim] for dim in order] for order in ORDERS]
    return core.astype(jnp.int32), places


def flip(value, part, step):
    return lax.ppermute(value, "fsdp", [(i, i ^ FLIP[ORDERS[part][step]]) for i in range(16)])


def swap(value):
    return lax.ppermute(value, "fsdp", SWAP_LAST)


def params(mib):
    return pltpu.CompilerParams(vmem_limit_bytes=mib * MIB)


def cost(flops, nbytes):
    return pl.CostEstimate(flops=flops, bytes_accessed=nbytes, transcendentals=0)


def pack_kernel(core_ref, rows_ref, out_ref):
    rows = rows_ref[...]

    def packed(core):
        pieces = []
        for part in PARTS:
            for chip in unit_order(part):
                at = 2 * UNIT * chip + UNIT * core + PART * part
                pieces.append(rows[:, at : at + PART])
        return jnp.concatenate(pieces, axis=1)

    @pl.when(core_ref[0] == 0)
    def _():
        out_ref[...] = packed(0)

    @pl.when(core_ref[0] == 1)
    def _():
        out_ref[...] = packed(1)


def pack(core, rows):
    tile = 256
    return pl.pallas_call(
        pack_kernel,
        grid_spec=pltpu.PrefetchScalarGridSpec(
            num_scalar_prefetch=1,
            grid=(TOK // tile,),
            in_specs=[pl.BlockSpec((tile, D), lambda i, s: (i, 0))],
            out_specs=pl.BlockSpec((tile, HALF), lambda i, s: (i, 0)),
        ),
        out_shape=jax.ShapeDtypeStruct((TOK, HALF), BF),
        compiler_params=params(14),
        cost_estimate=cost(0, 3 * TOK * D),
        name="pack",
    )(core, rows)


def turn_kernel(rows_ref, out_ref):
    out_ref[...] = rows_ref[...].T


def turn(rows):
    tile = 768
    return pl.pallas_call(
        turn_kernel,
        grid=(HALF // tile,),
        in_specs=[pl.BlockSpec((TOK, tile), lambda i: (0, i))],
        out_specs=pl.BlockSpec((tile, TOK), lambda i: (i, 0)),
        out_shape=jax.ShapeDtypeStruct((HALF, TOK), BF),
        compiler_params=params(8),
        cost_estimate=cost(0, 4 * TOK * HALF),
        name="turn",
    )(rows)


def dot(a, b):
    return jnp.dot(a, b, preferred_element_type=F32)


def product(refs):
    return sum(dot(refs[part][...], refs[3 + part][...]) for part in PARTS)


def project_near_kernel(at_ref, *refs):
    refs[-1][...] = product(refs)


def project_far_kernel(at_ref, *refs):
    refs[-1][...] = ((refs[-2][...] + product(refs)) * (1.0 / math.sqrt(D))).astype(BF)


def whole(*shape):
    return pl.BlockSpec(shape, lambda i, s: (0,) * len(shape))


def project(at, rows, quads, acc=None):
    near = acc is None

    def piece(part):
        return pl.BlockSpec((TOK, QUAD), lambda i, s: (0, s[part]))

    return pl.pallas_call(
        project_near_kernel if near else project_far_kernel,
        grid_spec=pltpu.PrefetchScalarGridSpec(
            num_scalar_prefetch=1,
            grid=(1,),
            in_specs=[piece(part) for part in PARTS]
            + [whole(QUAD, KVW)] * 3
            + ([] if near else [whole(TOK, KVW)]),
            out_specs=whole(TOK, KVW),
        ),
        out_shape=jax.ShapeDtypeStruct((TOK, KVW), F32 if near else BF),
        compiler_params=params(16),
        cost_estimate=cost(2 * TOK * KVW * 3 * QUAD, 7 * MIB),
        name="project_near" if near else "project_far",
    )(at, rows, rows, rows, *quads, *([] if near else [acc]))


def grad_kernel(at_ref, a_ref, b_ref, ra_ref, rb_ref, out_ref):
    out_ref[...] = (dot(a_ref[...], ra_ref[...]) + dot(b_ref[...], rb_ref[...])).astype(
        out_ref.dtype
    )


def grad_block(at, part, turned, residuals, dtype):
    piece = pl.BlockSpec((QUAD, TOK), lambda i, s: (s[part], 0))
    return pl.pallas_call(
        grad_kernel,
        grid_spec=pltpu.PrefetchScalarGridSpec(
            num_scalar_prefetch=1,
            grid=(1,),
            in_specs=[piece, piece, whole(TOK, KVW), whole(TOK, KVW)],
            out_specs=whole(QUAD, KVW),
        ),
        out_shape=jax.ShapeDtypeStruct((QUAD, KVW), dtype),
        compiler_params=params(12),
        cost_estimate=cost(4 * QUAD * KVW * TOK, 5 * MIB),
        name="grad",
    )(at, *turned, *residuals)


def inner_kernel(*refs):
    stay, came = refs[0:3], refs[3:6]
    w_ref, m_ref, v_ref, g_ref, m_out, v_out, w_out, delta_out = refs[6:]
    for part in PARTS:
        rows = slice(PART * part, PART * part + PART)
        grad = stay[part][...] + came[part][...].astype(F32)
        grad = grad * (1.0 / math.sqrt(TOK * 16))
        first = first_decay * m_ref[rows] + (1.0 - first_decay) * grad
        second = second_decay * v_ref[rows] + (1.0 - second_decay) * grad * grad
        m_out[rows] = first
        v_out[rows] = second
        wide = w_ref[rows].astype(F32)
        weight = (
            wide - inner_rate * (first / (jnp.sqrt(second) + adam_eps) + weight_decay * wide)
        ).astype(BF)
        w_out[rows] = weight
        delta = (g_ref[rows] - weight.astype(F32)).astype(BF)
        for group in range(delta_out.shape[0]):
            delta_out[group, rows] = delta[:, 128 * group : 128 * group + 128]


def inner(stay, came, weight, first, second, base):
    tile = 512
    piece = pl.BlockSpec((PART, tile), lambda i: (0, i))
    block = pl.BlockSpec((UNIT, tile), lambda i: (0, i))
    wide = jax.ShapeDtypeStruct((UNIT, KVW), F32)
    return pl.pallas_call(
        inner_kernel,
        grid=(KVW // tile,),
        in_specs=[piece] * 6 + [block] * 4,
        out_specs=[block, block, block, pl.BlockSpec((tile // 128, UNIT, 128), lambda i: (i, 0, 0))],
        out_shape=[
            wide,
            wide,
            jax.ShapeDtypeStruct((UNIT, KVW), BF),
            jax.ShapeDtypeStruct((KVW // 128, UNIT, 128), BF),
        ],
        compiler_params=params(16),
        cost_estimate=cost(20 * UNIT * KVW, 9 * MIB),
        name="inner",
    )(*stay, *came, weight, first, second, base)


def total_kernel(parts_ref, out_ref):
    out_ref[...] = jnp.sum(parts_ref[...].astype(F32), axis=0).astype(BF)


def totals(parts):
    return pl.pallas_call(
        total_kernel,
        out_shape=jax.ShapeDtypeStruct(parts.shape[1:], BF),
        compiler_params=params(8),
        cost_estimate=cost(0, MIB),
        name="totals",
    )(parts)


def replica_mean(delta):
    pieces = lax.all_to_all(delta, "replica", 0, 0, axis_index_groups=ALONG_Z)
    part = totals(pieces)
    other = lax.ppermute(part, "replica", SWAP_LAST)
    mean = ((part.astype(F32) + other.astype(F32)) * (1.0 / REPLICAS)).astype(BF)
    pieces = jnp.broadcast_to(mean[None], pieces.shape)
    return lax.all_to_all(pieces, "replica", 0, 0, axis_index_groups=ALONG_Z)


def outer_kernel(mean_ref, w_ref, g_ref, o_ref, local_out, global_out, momentum_out):
    groups = mean_ref.shape[0]
    mean = jnp.concatenate([mean_ref[group] for group in range(groups)], axis=1).astype(F32)
    momentum = outer_mu * o_ref[...] + mean
    base = g_ref[...] - outer_rate * (mean + outer_mu * momentum)
    momentum_out[...] = momentum
    global_out[...] = base
    local_out[...] = (mix_keep * w_ref[...].astype(F32) + (1.0 - mix_keep) * base).astype(BF)


def outer(mean, weight, base, momentum):
    tile = 512
    block = pl.BlockSpec((UNIT, tile), lambda i: (0, i))
    wide = jax.ShapeDtypeStruct((UNIT, KVW), F32)
    return pl.pallas_call(
        outer_kernel,
        grid=(KVW // tile,),
        in_specs=[pl.BlockSpec((tile // 128, UNIT, 128), lambda i: (i, 0, 0)), block, block, block],
        out_specs=[block, block, block],
        out_shape=[jax.ShapeDtypeStruct((UNIT, KVW), BF), wide, wide],
        compiler_params=params(16),
        cost_estimate=cost(8 * UNIT * KVW, 7 * MIB),
        name="outer",
    )(mean, weight, base, momentum)


def ordered(own_first, own, other):
    return jnp.where(
        own_first, jnp.concatenate([own, other], axis=0), jnp.concatenate([other, own], axis=0)
    )


def half_at(value, first):
    size = value.shape[0] // 2
    return jnp.where(first, value[:size], value[size:])


def local(
    tokens, targets, local_weights, first_moment, second_moment, global_weights, outer_momentum
):
    rows = tokens[0]
    wanted = targets[0]
    weight = local_weights[0]
    core, places = own_bits()
    near_at = jnp.stack([2 * part + places[part][2] for part in PARTS]).astype(jnp.int32)
    far_at = jnp.stack([2 * part + 1 - places[part][2] for part in PARTS]).astype(jnp.int32)

    lower = [[place == 0 for place in row] for row in places]
    upper = [[place != 0 for place in row] for row in places]
    core, near_at, far_at, lower, upper, weight, rows = lax.optimization_barrier(
        (core.reshape(1), near_at, far_at, lower, upper, weight, rows)
    )

    rows_other = swap(rows)
    held = [weight[PART * part : PART * part + PART] for part in PARTS]
    came = [flip(held[part], part, 0) for part in PARTS]
    held = [ordered(lower[part][0], held[part], came[part]) for part in PARTS]
    rows, held = lax.optimization_barrier((rows, held))
    came = [flip(held[part], part, 1) for part in PARTS]
    kept = pack(core, rows)
    came, kept, rows_other = lax.optimization_barrier((came, kept, rows_other))
    held = [ordered(lower[part][1], held[part], came[part]) for part in PARTS]
    far = [flip(held[part], part, 2) for part in PARTS]

    received = pack(core, rows_other)
    wanted_other = swap(wanted)
    turned = (turn(kept), turn(received))
    near_kept = project(near_at, kept, held)
    near_received = project(near_at, received, held)
    far, near_kept, near_received, turned, wanted_other = lax.optimization_barrier(
        (far, near_kept, near_received, turned, wanted_other)
    )
    own_received = project(far_at, received, far, near_received)
    cross_kept = swap(own_received)
    own_kept = project(far_at, kept, far, near_kept)
    cross_received = swap(own_kept)
    residuals = (
        (own_kept.astype(F32) + cross_kept.astype(F32) - wanted.astype(F32)).astype(BF),
        (own_received.astype(F32) + cross_received.astype(F32) - wanted_other.astype(F32)).astype(
            BF
        ),
    )

    came = [flip(grad_block(far_at, part, turned, residuals, BF), part, 2) for part in PARTS]
    sums = [grad_block(near_at, part, turned, residuals, F32) for part in PARTS]
    for step in (1, 0):
        sums = [sums[part] + came[part].astype(F32) for part in PARTS]
        came = [
            flip(half_at(sums[part], upper[part][step]).astype(BF), part, step)
            for part in PARTS
        ]
        sums = [half_at(sums[part], lower[part][step]) for part in PARTS]

    first, second, weight, delta = inner(
        sums, came, weight, first_moment[0], second_moment[0], global_weights
    )
    mean = replica_mean(delta)
    new_local, new_global, new_momentum = outer(mean, weight, global_weights, outer_momentum)
    return (new_local[None], first[None], second[None], new_global, new_momentum)


def solution(mesh):
    return jax.shard_map(
        local,
        mesh=mesh,
        in_specs=(
            P("replica", "fsdp", None),
            P("replica", "fsdp", None),
            P("replica", "fsdp", None),
            P("replica", "fsdp", None),
            P("replica", "fsdp", None),
            P("fsdp", None),
            P("fsdp", None),
        ),
        out_specs=(
            P("replica", "fsdp", None),
            P("replica", "fsdp", None),
            P("replica", "fsdp", None),
            P("fsdp", None),
            P("fsdp", None),
        ),
        check_vma=False,
    )
```

time: 176 us -> 155 us (0.88)
  local copies, waits for them, and re-layouts: 18.9 us -> 3.68 us
  Pallas kernels: 39.7 us -> 27.6 us
  waiting for transfers between devices: 36.4 us -> 44.3 us
  blocking collectives: 46.6 us -> 41.9 us
  starting transfers between devices: 27.9 us -> 31.8 us
    dynamic_update_slice x12 -> x0, local copies, waits for them, and re-layouts: 10.7 us -> none  [the longest x6 5.76 us: ordered(): return lax.dynamic_update_slice(out, other, ((1 - bit) * size, 0))]
    pallas_call x7, Pallas kernels: 24.1 us -> 14.1 us  [the longest x4 9.38 us: project(): pl.pallas_call(project_near_kernel if near else project_far_kernel, grid_...]
    ppermute x22 -> x23, waiting for transfers between devices: 36.4 us -> 44.3 us  [the longest x18 39 us: flip(): lax.ppermute(value, 'fsdp', [(i, i ^ FLIP[ORDERS[part][step]]) for i in r...]
    all_to_all x2, blocking collectives: 46.6 us -> 41.9 us  [the longest x1 24.8 us: replica_mean(): pieces = lax.all_to_all(delta, 'replica', 0, 0, axis_index_groups=ALONG_Z)]
    ppermute x22 -> x23, starting transfers between devices: 27.9 us -> 31.8 us  [the longest x18 30.3 us: flip(): lax.ppermute(value, 'fsdp', [(i, i ^ FLIP[ORDERS[part][step]]) for i in r...]
    another operation x6 -> x0, local copies, waits for them, and re-layouts: 3.64 us -> none
    pallas_call x2, Pallas kernels: 4.95 us -> 1.97 us  [turn(): pl.pallas_call(turn_kernel, grid=(HALF // tile,), in_specs=[pl.BlockSpec(...]
    convert_element_type x2 -> x9, other arithmetic: 3.57 us -> 1.66 us  [the longest x1 0.65 us: local(): (own_kept.astype(F32) + cross_kept.astype(F32) - wanted.astype(F32)).asty...]
  transfers between devices with their start and end apart: 22 -> 23, of which waited for: 10 -> 18; matrix products, arithmetic and copies ran while one was open for 10% -> 3% of each run, Pallas kernels for 19% -> 12%
where the time goes in v2:
time: 155 us; the launch traced here: 154 us
  waiting for transfers between devices  44.3 us (29%)
  blocking collectives  41.9 us (27%)
  starting transfers between devices  31.8 us (21%)
  Pallas kernels  27.6 us (18%)
  other arithmetic  4.23 us (3%)
  local copies, waits for them, and re-layouts  3.68 us (2%)
    ppermute x18, waiting for transfers between devices, flip(): lax.ppermute(value, 'fsdp', [(i, i ^ FLIP[ORDERS[part][step]]) for i in r...  39 us
    ppermute x18, starting transfers between devices, flip(): lax.ppermute(value, 'fsdp', [(i, i ^ FLIP[ORDERS[part][step]]) for i in r...  30.3 us
    all_to_all x1, blocking collectives, replica_mean(): pieces = lax.all_to_all(delta, 'replica', 0, 0, axis_index_groups=ALONG_Z)  24.8 us
    all_to_all x1, blocking collectives, replica_mean(): return lax.all_to_all(pieces, 'replica', 0, 0, axis_index_groups=ALONG_Z)  17 us
    pallas_call x4, Pallas kernels, project(): pl.pallas_call(project_near_kernel if near else project_far_kernel, grid_...  9.38 us
    pallas_call x6, Pallas kernels, grad_block(): pl.pallas_call(grad_kernel, grid_spec=pltpu.PrefetchScalarGridSpec(num_sc...  9.07 us
    ppermute x1, waiting for transfers between devices, replica_mean(): other = lax.ppermute(part, 'replica', SWAP_LAST)  3.68 us
  transfers between devices with their start and end apart: 23, of which 18 were waited for; matrix products, arithmetic and copies ran while one was open for 3% of the time, Pallas kernels for 12%

profile of v2, /device:TPU:2, one launch (start us, length us, event | category | flops | bytes accessed | tf_op | source)
XLA Modules:
  0.0 154.5 jit_solution(12719446857865156623)
XLA Ops:
  2.0 3.3 %collective-permute-start.2 = (bf16[96,1024]{1,0:T(8,128)(2,1)S(1)}, bf16[96,1024]{1,0:T(8,128)(2,1)S(1)}, u32[]{:S(2)}, u32[]{:S(2)}) collective-permute-start(bf16[96,1024]{1,0:T(8,128)(2,1)S(1)} %get-tuple-element.87), channel_id=1, source_target_pairs={{0,8},{1,9},{2,10},{3,11},{4,12},{5,13},{6,14},{7,15},{8,0},{9,1},... | collective-permute-start | bytes 589832 | tf_op jit(solution)/shard_map/ppermute | solution.py:66
  8.6 2.3 %collective-permute-done.2 = bf16[96,1024]{1,0:T(8,128)(2,1)S(1)} collective-permute-done((bf16[96,1024]{1,0:T(8,128)(2,1)S(1)}, bf16[96,1024]{1,0:T(8,128)(2,1)S(1)}, u32[]{:S(2)}, u32[]{:S(2)}) %collective-permute-start.2) | collective-permute-done | bytes 196640 | tf_op jit(solution)/shard_map/ppermute | solution.py:66
  15.9 2.1 %collective-permute-start.5 = (bf16[192,1024]{1,0:T(8,128)(2,1)S(1)}, bf16[192,1024]{1,0:T(8,128)(2,1)S(1)}, u32[]{:S(2)}, u32[]{:S(2)}) collective-permute-start(bf16[192,1024]{1,0:T(8,128)(2,1)S(1)} %maximum_select_fusion.5), channel_id=1, source_target_pairs={{0,2},{1,3},{2,0},{3,1},{4,6},{5,7},{6,4},{7,5},{8,10},{9,11},{10,... | collective-permute-start | bytes 1179656 | tf_op jit(solution)/shard_map/ppermute | solution.py:66
  18.0 2.3 %copy-done = bf16[1,512,4608]{2,1,0:T(8,128)(2,1)S(1)} copy-done((bf16[1,512,4608]{2,1,0:T(8,128)(2,1)S(1)}, bf16[1,512,4608]{2,1,0:T(8,128)(2,1)}, u32[]{:S(2)}) %copy-start) | copy-done | bytes 4718616
  21.6 2.2 %collective-permute-done.3 = bf16[192,1024]{1,0:T(8,128)(2,1)S(1)} collective-permute-done((bf16[192,1024]{1,0:T(8,128)(2,1)S(1)}, bf16[192,1024]{1,0:T(8,128)(2,1)S(1)}, u32[]{:S(2)}, u32[]{:S(2)}) %collective-permute-start.3) | collective-permute-done | bytes 393248 | tf_op jit(solution)/shard_map/ppermute | solution.py:66
  27.7 3.0 %collective-permute-start.8 = (bf16[384,1024]{1,0:T(8,128)(2,1)S(1)}, bf16[384,1024]{1,0:T(8,128)(2,1)S(1)}, u32[]{:S(2)}, u32[]{:S(2)}) collective-permute-start(bf16[384,1024]{1,0:T(8,128)(2,1)S(1)} %maximum_select_fusion.1.refs_4_), channel_id=1, source_target_pairs={{0,2},{1,3},{2,0},{3,1},{4,6},{5,7},{6,4},{7,5},{8,10},{9,11},{10,... | collective-permute-start | bytes 2359304 | tf_op jit(solution)/shard_map/ppermute | solution.py:66
  31.0 2.0 %collective-permute-start.7 = (bf16[384,1024]{1,0:T(8,128)(2,1)S(1)}, bf16[384,1024]{1,0:T(8,128)(2,1)S(1)}, u32[]{:S(2)}, u32[]{:S(2)}) collective-permute-start(bf16[384,1024]{1,0:T(8,128)(2,1)S(1)} %maximum_select_fusion.refs_3_), channel_id=1, source_target_pairs={{0,8},{1,9},{2,10},{3,11},{4,12},{5,13},{6,14},{7,15},{8,0},{9,1},... | collective-permute-start | bytes 2359304 | tf_op jit(solution)/shard_map/ppermute | solution.py:66
  36.3 2.3 %project_near.2.refs_6_ = f32[512,1024]{1,0:T(8,128)S(1)} custom-call(s32[3]{0:T(128)S(1)} %get-tuple-element.48.at_ref, bf16[512,2304]{1,0:T(8,128)(2,1)S(1)} %pack.2.refs_0_.refs_1_.refs_2_.rows_ref, bf16[512,2304]{1,0:T(8,128)(2,1)S(1)} %pack.2.refs_0_.refs_1_.refs_2_.rows_ref, bf16[512,2304]{1,0:T(8,128)(2,1)S(1)} %pack.2.refs_0_.refs_1_.refs_2_.rows_ref, ...), custom_call_target="tpu_custom_call" | custom-call | flops 1207959552 | bytes 7340032 | tf_op jit(solution)/shard_map/project_near/pallas_call | solution.py:162
  38.6 2.3 %project_near.3.refs_6_ = f32[512,1024]{1,0:T(8,128)S(1)} custom-call(s32[3]{0:T(128)S(1)} %get-tuple-element.48.at_ref, bf16[512,2304]{1,0:T(8,128)(2,1)S(1)} %pack.3.refs_0_.refs_1_.refs_2_.rows_ref, bf16[512,2304]{1,0:T(8,128)(2,1)S(1)} %pack.3.refs_0_.refs_1_.refs_2_.rows_ref, bf16[512,2304]{1,0:T(8,128)(2,1)S(1)} %pack.3.refs_0_.refs_1_.refs_2_.rows_ref, ...), custom_call_target="tpu_custom_call" | custom-call | flops 1207959552 | bytes 7340032 | tf_op jit(solution)/shard_map/project_near/pallas_call | solution.py:162
  41.0 3.1 %collective-permute-done.9.refs_5_ = bf16[384,1024]{1,0:T(8,128)(2,1)S(1)} collective-permute-done((bf16[384,1024]{1,0:T(8,128)(2,1)S(1)}, bf16[384,1024]{1,0:T(8,128)(2,1)S(1)}, u32[]{:S(2)}, u32[]{:S(2)}) %collective-permute-start.9) | collective-permute-done | bytes 786464 | tf_op jit(solution)/shard_map/ppermute | solution.py:66
  45.9 3.5 %collective-permute-done.7.refs_3_ = bf16[384,1024]{1,0:T(8,128)(2,1)S(1)} collective-permute-done((bf16[384,1024]{1,0:T(8,128)(2,1)S(1)}, bf16[384,1024]{1,0:T(8,128)(2,1)S(1)}, u32[]{:S(2)}, u32[]{:S(2)}) %collective-permute-start.7) | collective-permute-done | bytes 786464 | tf_op jit(solution)/shard_map/ppermute | solution.py:66
  49.5 2.4 %project_far.3 = bf16[512,1024]{1,0:T(8,128)(2,1)S(1)} custom-call(s32[3]{0:T(128)S(1)} %get-tuple-element.67.at_ref, bf16[512,2304]{1,0:T(8,128)(2,1)S(1)} %pack.3.refs_0_.refs_1_.refs_2_.rows_ref, bf16[512,2304]{1,0:T(8,128)(2,1)S(1)} %pack.3.refs_0_.refs_1_.refs_2_.rows_ref, bf16[512,2304]{1,0:T(8,128)(2,1)S(1)} %pack.3.refs_0_.refs_1_.refs_2_.rows_ref, ...), custom_call_target="tpu_custom_call" | custom-call | flops 1207959552 | bytes 7340032 | tf_op jit(solution)/shard_map/project_far/pallas_call | solution.py:162
  51.9 2.3 %project_far.2 = bf16[512,1024]{1,0:T(8,128)(2,1)S(1)} custom-call(s32[3]{0:T(128)S(1)} %get-tuple-element.67.at_ref, bf16[512,2304]{1,0:T(8,128)(2,1)S(1)} %pack.2.refs_0_.refs_1_.refs_2_.rows_ref, bf16[512,2304]{1,0:T(8,128)(2,1)S(1)} %pack.2.refs_0_.refs_1_.refs_2_.rows_ref, bf16[512,2304]{1,0:T(8,128)(2,1)S(1)} %pack.2.refs_0_.refs_1_.refs_2_.rows_ref, ...), custom_call_target="tpu_custom_call" | custom-call | flops 1207959552 | bytes 7340032 | tf_op jit(solution)/shard_map/project_far/pallas_call | solution.py:162
  71.4 7.8 %collective-permute-done.17 = bf16[384,1024]{1,0:T(8,128)(2,1)S(1)} collective-permute-done((bf16[384,1024]{1,0:T(8,128)(2,1)S(1)}, bf16[384,1024]{1,0:T(8,128)(2,1)S(1)}, u32[]{:S(2)}, u32[]{:S(2)}) %collective-permute-start.17) | collective-permute-done | bytes 786464 | tf_op jit(solution)/shard_map/ppermute | solution.py:66
  81.1 2.6 %collective-permute-done.13 = bf16[384,1024]{1,0:T(8,128)(2,1)S(1)} collective-permute-done((bf16[384,1024]{1,0:T(8,128)(2,1)S(1)}, bf16[384,1024]{1,0:T(8,128)(2,1)S(1)}, u32[]{:S(2)}, u32[]{:S(2)}) %collective-permute-start.13) | collective-permute-done | bytes 786464 | tf_op jit(solution)/shard_map/ppermute | solution.py:66
  86.7 2.2 %collective-permute-start.16 = (bf16[192,1024]{1,0:T(8,128)(2,1)S(1)}, bf16[192,1024]{1,0:T(8,128)(2,1)S(1)}, u32[]{:S(2)}, u32[]{:S(2)}) collective-permute-start(bf16[192,1024]{1,0:T(8,128)(2,1)S(1)} %select_convert_fusion.1), channel_id=1, source_target_pairs={{0,8},{1,9},{2,10},{3,11},{4,12},{5,13},{6,14},{7,15},{8,0},{9,1},... | collective-permute-start | bytes 1179656 | tf_op jit(solution)/shard_map/ppermute | solution.py:66
  88.9 4.7 %collective-permute-done.18 = bf16[192,1024]{1,0:T(8,128)(2,1)S(1)} collective-permute-done((bf16[192,1024]{1,0:T(8,128)(2,1)S(1)}, bf16[192,1024]{1,0:T(8,128)(2,1)S(1)}, u32[]{:S(2)}, u32[]{:S(2)}) %collective-permute-start.18) | collective-permute-done | bytes 393248 | tf_op jit(solution)/shard_map/ppermute | solution.py:66
  93.8 2.2 %collective-permute-start.21 = (bf16[96,1024]{1,0:T(8,128)(2,1)S(1)}, bf16[96,1024]{1,0:T(8,128)(2,1)S(1)}, u32[]{:S(2)}, u32[]{:S(2)}) collective-permute-start(bf16[96,1024]{1,0:T(8,128)(2,1)S(1)} %select_convert_fusion.3), channel_id=1, source_target_pairs={{0,8},{1,9},{2,10},{3,11},{4,12},{5,13},{6,14},{7,15},{8,0},{9,1},... | collective-permute-start | bytes 589832 | tf_op jit(solution)/shard_map/ppermute | solution.py:66
  99.1 2.2 %collective-permute-done.21.refs_5_ = bf16[96,1024]{1,0:T(8,128)(2,1)S(1)} collective-permute-done((bf16[96,1024]{1,0:T(8,128)(2,1)S(1)}, bf16[96,1024]{1,0:T(8,128)(2,1)S(1)}, u32[]{:S(2)}, u32[]{:S(2)}) %collective-permute-start.21) | collective-permute-done | bytes 196640 | tf_op jit(solution)/shard_map/ppermute | solution.py:66
  103.4 2.6 %inner.1 = (f32[288,1024]{1,0:T(8,128)}, f32[288,1024]{1,0:T(8,128)}, bf16[288,1024]{1,0:T(8,128)(2,1)S(1)}, bf16[8,288,128]{2,1,0:T(8,128)(2,1)S(1)}) custom-call(f32[96,1024]{1,0:T(8,128)S(1)} %slice_select_fusion.2.refs_0_, f32[96,1024]{1,0:T(8,128)S(1)} %slice_select_fusion.1.refs_1_, f32[96,1024]{1,0:T(8,128)S(1)} %slice_select_fusion.refs_2_, ...), custom_call_target="tpu_custom_call" | custom-call | flops 5898240 | bytes 9437184 | tf_op jit(solution)/shard_map/inner/pallas_call | solution.py:228
  106.0 24.8 %all_to_all.10.parts_ref = bf16[8,288,128]{2,1,0:T(8,128)(2,1)S(1)} all-to-all(bf16[8,288,128]{2,1,0:T(8,128)(2,1)S(1)} %get-tuple-element.80), channel_id=1, replica_groups={{0,32,64,96,128,160,192,224},{16,48,80,112,144,176,208,240},{1,33,65,97..., dimensions={0} | all-to-all | bytes 1179648 | tf_op jit(solution)/shard_map/all_to_all | solution.py:260
  131.7 3.7 %collective-permute-done.22 = bf16[288,128]{1,0:T(8,128)(2,1)S(1)} collective-permute-done((bf16[288,128]{1,0:T(8,128)(2,1)S(1)}, bf16[288,128]{1,0:T(8,128)(2,1)S(1)}, u32[]{:S(2)}, u32[]{:S(2)}) %collective-permute-start.22) | collective-permute-done | bytes 73760 | tf_op jit(solution)/shard_map/ppermute | solution.py:262
  135.5 17.0 %all_to_all.11.mean_ref = bf16[8,288,128]{2,1,0:T(8,128)(2,1)S(1)} all-to-all(bf16[8,288,128]{2,1,0:T(8,128)(2,1)S(1)} %broadcast_in_dim.15), channel_id=1, replica_groups={{0,32,64,96,128,160,192,224},{16,48,80,112,144,176,208,240},{1,33,65,97..., dimensions={0} | all-to-all | bytes 1179648 | tf_op jit(solution)/shard_map/all_to_all | solution.py:265
  152.5 2.0 %outer.1 = (bf16[288,1024]{1,0:T(8,128)(2,1)}, f32[288,1024]{1,0:T(8,128)}, f32[288,1024]{1,0:T(8,128)}) custom-call(bf16[8,288,128]{2,1,0:T(8,128)(2,1)S(1)} %all_to_all.11.mean_ref, bf16[288,1024]{1,0:T(8,128)(2,1)S(1)} %get-tuple-element.81.w_ref, f32[288,1024]{1,0:T(8,128)S(1)} %copy-done.1, f32[288,1024]{1,0:T(8,128)S(1)} %copy-done.3), custom_call_target="tpu_custom_call" | custom-call | flops 2359296 | bytes 7340032 | tf_op jit(solution)/shard_map/outer/pallas_call | solution.py:282
  (82 shorter events, 48.6 us)
Async XLA Ops:
  0.7 25.3 %collective-permute-start.6 = (bf16[512,4608]{1,0:T(8,128)(2,1)}, bf16[512,4608]{1,0:T(8,128)(2,1)S(1)}, u32[]{:S(2)}, u32[]{:S(2)}) collective-permute-start(bf16[512,4608]{1,0:T(8,128)(2,1)} %bitcast.16), channel_id=1, source_target_pairs={{0,1},{1,0},{2,3},{3,2},{4,5},{5,4},{6,7},{7,6},{8,9},{9,8},{10,11... | collective-permute-start | bytes 14155784 | tf_op jit(solution)/shard_map/ppermute | solution.py:70
  2.0 8.8 %collective-permute-start.2 = (bf16[96,1024]{1,0:T(8,128)(2,1)S(1)}, bf16[96,1024]{1,0:T(8,128)(2,1)S(1)}, u32[]{:S(2)}, u32[]{:S(2)}) collective-permute-start(bf16[96,1024]{1,0:T(8,128)(2,1)S(1)} %get-tuple-element.87), channel_id=1, source_target_pairs={{0,8},{1,9},{2,10},{3,11},{4,12},{5,13},{6,14},{7,15},{8,0},{9,1},... | collective-permute-start | bytes 589832 | tf_op jit(solution)/shard_map/ppermute | solution.py:66
  5.3 7.0 %collective-permute-start.1 = (bf16[96,1024]{1,0:T(8,128)(2,1)S(1)}, bf16[96,1024]{1,0:T(8,128)(2,1)S(1)}, u32[]{:S(2)}, u32[]{:S(2)}) collective-permute-start(bf16[96,1024]{1,0:T(8,128)(2,1)S(1)} %get-tuple-element.88), channel_id=1, source_target_pairs={{0,6},{1,7},{2,4},{3,5},{4,2},{5,3},{6,0},{7,1},{8,14},{9,15},{10,... | collective-permute-start | bytes 589832 | tf_op jit(solution)/shard_map/ppermute | solution.py:66
  6.8 6.7 %collective-permute-start = (bf16[96,1024]{1,0:T(8,128)(2,1)S(1)}, bf16[96,1024]{1,0:T(8,128)(2,1)S(1)}, u32[]{:S(2)}, u32[]{:S(2)}) collective-permute-start(bf16[96,1024]{1,0:T(8,128)(2,1)S(1)} %get-tuple-element.89), channel_id=1, source_target_pairs={{0,2},{1,3},{2,0},{3,1},{4,6},{5,7},{6,4},{7,5},{8,10},{9,11},{10,... | collective-permute-start | bytes 589832 | tf_op jit(solution)/shard_map/ppermute | solution.py:66
  13.6 10.2 %collective-permute-start.3 = (bf16[192,1024]{1,0:T(8,128)(2,1)S(1)}, bf16[192,1024]{1,0:T(8,128)(2,1)S(1)}, u32[]{:S(2)}, u32[]{:S(2)}) collective-permute-start(bf16[192,1024]{1,0:T(8,128)(2,1)S(1)} %maximum_select_fusion.3), channel_id=1, source_target_pairs={{0,6},{1,7},{2,4},{3,5},{4,2},{5,3},{6,0},{7,1},{8,14},{9,15},{10,... | collective-permute-start | bytes 1179656 | tf_op jit(solution)/shard_map/ppermute | solution.py:66
  14.2 11.4 %collective-permute-start.4 = (bf16[192,1024]{1,0:T(8,128)(2,1)S(1)}, bf16[192,1024]{1,0:T(8,128)(2,1)S(1)}, u32[]{:S(2)}, u32[]{:S(2)}) collective-permute-start(bf16[192,1024]{1,0:T(8,128)(2,1)S(1)} %maximum_select_fusion.4), channel_id=1, source_target_pairs={{0,8},{1,9},{2,10},{3,11},{4,12},{5,13},{6,14},{7,15},{8,0},{9,1},... | collective-permute-start | bytes 1179656 | tf_op jit(solution)/shard_map/ppermute | solution.py:66
  15.9 10.2 %collective-permute-start.5 = (bf16[192,1024]{1,0:T(8,128)(2,1)S(1)}, bf16[192,1024]{1,0:T(8,128)(2,1)S(1)}, u32[]{:S(2)}, u32[]{:S(2)}) collective-permute-start(bf16[192,1024]{1,0:T(8,128)(2,1)S(1)} %maximum_select_fusion.5), channel_id=1, source_target_pairs={{0,2},{1,3},{2,0},{3,1},{4,6},{5,7},{6,4},{7,5},{8,10},{9,11},{10,... | collective-permute-start | bytes 1179656 | tf_op jit(solution)/shard_map/ppermute | solution.py:66
  18.0 23.0 %collective-permute-start.10 = (bf16[512,1024]{1,0:T(8,128)(2,1)S(1)}, bf16[512,1024]{1,0:T(8,128)(2,1)S(1)}, u32[]{:S(2)}, u32[]{:S(2)}) collective-permute-start(bf16[512,1024]{1,0:T(8,128)(2,1)S(1)} %bitcast.22), channel_id=1, source_target_pairs={{0,1},{1,0},{2,3},{3,2},{4,5},{5,4},{6,7},{7,6},{8,9},{9,8},{10,11... | collective-permute-start | bytes 3145736 | tf_op jit(solution)/shard_map/ppermute | solution.py:70
  26.4 17.7 %collective-permute-start.9 = (bf16[384,1024]{1,0:T(8,128)(2,1)S(1)}, bf16[384,1024]{1,0:T(8,128)(2,1)S(1)}, u32[]{:S(2)}, u32[]{:S(2)}) collective-permute-start(bf16[384,1024]{1,0:T(8,128)(2,1)S(1)} %maximum_select_fusion.2.refs_5_), channel_id=1, source_target_pairs={{0,6},{1,7},{2,4},{3,5},{4,2},{5,3},{6,0},{7,1},{8,14},{9,15},{10,... | collective-permute-start | bytes 2359304 | tf_op jit(solution)/shard_map/ppermute | solution.py:66
  27.7 18.2 %collective-permute-start.8 = (bf16[384,1024]{1,0:T(8,128)(2,1)S(1)}, bf16[384,1024]{1,0:T(8,128)(2,1)S(1)}, u32[]{:S(2)}, u32[]{:S(2)}) collective-permute-start(bf16[384,1024]{1,0:T(8,128)(2,1)S(1)} %maximum_select_fusion.1.refs_4_), channel_id=1, source_target_pairs={{0,2},{1,3},{2,0},{3,1},{4,6},{5,7},{6,4},{7,5},{8,10},{9,11},{10,... | collective-permute-start | bytes 2359304 | tf_op jit(solution)/shard_map/ppermute | solution.py:66
  31.0 18.5 %collective-permute-start.7 = (bf16[384,1024]{1,0:T(8,128)(2,1)S(1)}, bf16[384,1024]{1,0:T(8,128)(2,1)S(1)}, u32[]{:S(2)}, u32[]{:S(2)}) collective-permute-start(bf16[384,1024]{1,0:T(8,128)(2,1)S(1)} %maximum_select_fusion.refs_3_), channel_id=1, source_target_pairs={{0,8},{1,9},{2,10},{3,11},{4,12},{5,13},{6,14},{7,15},{8,0},{9,1},... | collective-permute-start | bytes 2359304 | tf_op jit(solution)/shard_map/ppermute | solution.py:66
  51.8 3.0 %collective-permute-start.11 = (bf16[512,1024]{1,0:T(8,128)(2,1)S(1)}, bf16[512,1024]{1,0:T(8,128)(2,1)S(1)}, u32[]{:S(2)}, u32[]{:S(2)}) collective-permute-start(bf16[512,1024]{1,0:T(8,128)(2,1)S(1)} %project_far.3), channel_id=1, source_target_pairs={{0,1},{1,0},{2,3},{3,2},{4,5},{5,4},{6,7},{7,6},{8,9},{9,8},{10,11... | collective-permute-start | bytes 3145736 | tf_op jit(solution)/shard_map/ppermute | solution.py:70
  54.3 2.9 %collective-permute-start.12 = (bf16[512,1024]{1,0:T(8,128)(2,1)S(1)}, bf16[512,1024]{1,0:T(8,128)(2,1)S(1)}, u32[]{:S(2)}, u32[]{:S(2)}) collective-permute-start(bf16[512,1024]{1,0:T(8,128)(2,1)S(1)} %project_far.2), channel_id=1, source_target_pairs={{0,1},{1,0},{2,3},{3,2},{4,5},{5,4},{6,7},{7,6},{8,9},{9,8},{10,11... | collective-permute-start | bytes 3145736 | tf_op jit(solution)/shard_map/ppermute | solution.py:70
  59.3 19.9 %collective-permute-start.17 = (bf16[384,1024]{1,0:T(8,128)(2,1)S(1)}, bf16[384,1024]{1,0:T(8,128)(2,1)S(1)}, u32[]{:S(2)}, u32[]{:S(2)}) collective-permute-start(bf16[384,1024]{1,0:T(8,128)(2,1)S(1)} %grad.11), channel_id=1, source_target_pairs={{0,6},{1,7},{2,4},{3,5},{4,2},{5,3},{6,0},{7,1},{8,14},{9,15},{10,... | collective-permute-start | bytes 2359304 | tf_op jit(solution)/shard_map/ppermute | solution.py:66
  62.6 21.1 %collective-permute-start.13 = (bf16[384,1024]{1,0:T(8,128)(2,1)S(1)}, bf16[384,1024]{1,0:T(8,128)(2,1)S(1)}, u32[]{:S(2)}, u32[]{:S(2)}) collective-permute-start(bf16[384,1024]{1,0:T(8,128)(2,1)S(1)} %grad.7), channel_id=1, source_target_pairs={{0,8},{1,9},{2,10},{3,11},{4,12},{5,13},{6,14},{7,15},{8,0},{9,1},... | collective-permute-start | bytes 2359304 | tf_op jit(solution)/shard_map/ppermute | solution.py:66
  65.6 20.7 %collective-permute-start.15 = (bf16[384,1024]{1,0:T(8,128)(2,1)S(1)}, bf16[384,1024]{1,0:T(8,128)(2,1)S(1)}, u32[]{:S(2)}, u32[]{:S(2)}) collective-permute-start(bf16[384,1024]{1,0:T(8,128)(2,1)S(1)} %grad.9), channel_id=1, source_target_pairs={{0,2},{1,3},{2,0},{3,1},{4,6},{5,7},{6,4},{7,5},{8,10},{9,11},{10,... | collective-permute-start | bytes 2359304 | tf_op jit(solution)/shard_map/ppermute | solution.py:66
  79.5 14.1 %collective-permute-start.18 = (bf16[192,1024]{1,0:T(8,128)(2,1)S(1)}, bf16[192,1024]{1,0:T(8,128)(2,1)S(1)}, u32[]{:S(2)}, u32[]{:S(2)}) collective-permute-start(bf16[192,1024]{1,0:T(8,128)(2,1)S(1)} %select_convert_fusion), channel_id=1, source_target_pairs={{0,2},{1,3},{2,0},{3,1},{4,6},{5,7},{6,4},{7,5},{8,10},{9,11},{10,... | collective-permute-start | bytes 1179656 | tf_op jit(solution)/shard_map/ppermute | solution.py:66
  84.0 11.9 %collective-permute-start.14 = (bf16[192,1024]{1,0:T(8,128)(2,1)S(1)}, bf16[192,1024]{1,0:T(8,128)(2,1)S(1)}, u32[]{:S(2)}, u32[]{:S(2)}) collective-permute-start(bf16[192,1024]{1,0:T(8,128)(2,1)S(1)} %select_convert_fusion.2), channel_id=1, source_target_pairs={{0,6},{1,7},{2,4},{3,5},{4,2},{5,3},{6,0},{7,1},{8,14},{9,15},{10,... | collective-permute-start | bytes 1179656 | tf_op jit(solution)/shard_map/ppermute | solution.py:66
  86.7 10.6 %collective-permute-start.16 = (bf16[192,1024]{1,0:T(8,128)(2,1)S(1)}, bf16[192,1024]{1,0:T(8,128)(2,1)S(1)}, u32[]{:S(2)}, u32[]{:S(2)}) collective-permute-start(bf16[192,1024]{1,0:T(8,128)(2,1)S(1)} %select_convert_fusion.1), channel_id=1, source_target_pairs={{0,8},{1,9},{2,10},{3,11},{4,12},{5,13},{6,14},{7,15},{8,0},{9,1},... | collective-permute-start | bytes 1179656 | tf_op jit(solution)/shard_map/ppermute | solution.py:66
  93.8 7.5 %collective-permute-start.21 = (bf16[96,1024]{1,0:T(8,128)(2,1)S(1)}, bf16[96,1024]{1,0:T(8,128)(2,1)S(1)}, u32[]{:S(2)}, u32[]{:S(2)}) collective-permute-start(bf16[96,1024]{1,0:T(8,128)(2,1)S(1)} %select_convert_fusion.3), channel_id=1, source_target_pairs={{0,8},{1,9},{2,10},{3,11},{4,12},{5,13},{6,14},{7,15},{8,0},{9,1},... | collective-permute-start | bytes 589832 | tf_op jit(solution)/shard_map/ppermute | solution.py:66
  96.2 5.8 %collective-permute-start.19 = (bf16[96,1024]{1,0:T(8,128)(2,1)S(1)}, bf16[96,1024]{1,0:T(8,128)(2,1)S(1)}, u32[]{:S(2)}, u32[]{:S(2)}) collective-permute-start(bf16[96,1024]{1,0:T(8,128)(2,1)S(1)} %select_convert_fusion.5), channel_id=1, source_target_pairs={{0,2},{1,3},{2,0},{3,1},{4,6},{5,7},{6,4},{7,5},{8,10},{9,11},{10,... | collective-permute-start | bytes 589832 | tf_op jit(solution)/shard_map/ppermute | solution.py:66
  97.6 5.8 %collective-permute-start.20 = (bf16[96,1024]{1,0:T(8,128)(2,1)S(1)}, bf16[96,1024]{1,0:T(8,128)(2,1)S(1)}, u32[]{:S(2)}, u32[]{:S(2)}) collective-permute-start(bf16[96,1024]{1,0:T(8,128)(2,1)S(1)} %select_convert_fusion.4), channel_id=1, source_target_pairs={{0,6},{1,7},{2,4},{3,5},{4,2},{5,3},{6,0},{7,1},{8,14},{9,15},{10,... | collective-permute-start | bytes 589832 | tf_op jit(solution)/shard_map/ppermute | solution.py:66
  130.8 21.7 %copy-start.3 = (f32[288,1024]{1,0:T(8,128)S(1)}, f32[288,1024]{1,0:T(8,128)}, u32[]{:S(2)}) copy-start(f32[288,1024]{1,0:T(8,128)} %o_ref.1) | copy-start | bytes 3538948
  130.9 4.4 %collective-permute-start.22 = (bf16[288,128]{1,0:T(8,128)(2,1)S(1)}, bf16[288,128]{1,0:T(8,128)(2,1)S(1)}, u32[]{:S(2)}, u32[]{:S(2)}) collective-permute-start(bf16[288,128]{1,0:T(8,128)(2,1)S(1)} %totals.1), channel_id=1, source_target_pairs={{0,16},{16,0},{32,48},{48,32},{64,80},{80,64},{96,112},{112,96},{1... | collective-permute-start | bytes 221192 | tf_op jit(solution)/shard_map/ppermute | solution.py:262
  (6 other events, 43.3 us)

commit v3 on v2

v3 whole, which is shorter than its diff:
```python
import math

import jax
import jax.numpy as jnp
from jax import lax
from jax.experimental import pallas as pl
from jax.experimental.pallas import tpu as pltpu
from jax.sharding import PartitionSpec as P

inner_rate = 0.02
first_decay = 0.5
second_decay = 0.95
adam_eps = 1e-08
weight_decay = 0.1
outer_rate = 0.7
outer_mu = 0.9
mix_keep = 0.5

BF = jnp.bfloat16
F32 = jnp.float32

D = 4608
KVW = 1024
TOK = 512
UNIT = 288
HALF = 2304
REPLICAS = 16
MIB = 1024 * 1024

EVEN, ODD, WIDE = 1, 2, 4
ORDER = (0, EVEN, ODD, WIDE, EVEN | ODD, ODD | WIDE, EVEN | WIDE, EVEN | ODD | WIDE)
CHIP_FLIP = {EVEN: 1, ODD: 3, WIDE: 4}
PART = 96
PAIR = 2 * PART
QUAD = 4 * PART
PARTS = range(3)
ORDERS = ((ODD, WIDE, EVEN), (EVEN, ODD, WIDE), (WIDE, EVEN, ODD))
FIRST = 4 * UNIT
SWAP_LAST = [(i, i ^ 1) for i in range(16)]
ALONG_Z = [list(range(0, 16, 2)), list(range(1, 16, 2))]


SENT = {dim: [] for dim in (EVEN, ODD, WIDE)}
for part_of, (one, two, three) in enumerate(ORDERS):
    SENT[two].append((one, part_of))
    SENT[three] += [(one, part_of), (two, part_of)]


def chip_mask(away):
    mask = 0
    for dim, flipped in CHIP_FLIP.items():
        if away & dim:
            mask ^= flipped
    return mask


def rows_of(away, part):
    at = UNIT * ORDER.index(away) + PART * part
    return slice(at, at + PART)


def flip(value, dim):
    return lax.ppermute(value, "fsdp", [(i, i ^ (2 * CHIP_FLIP[dim])) for i in range(16)])


def swap(value):
    return lax.ppermute(value, "fsdp", SWAP_LAST)


def params(mib):
    return pltpu.CompilerParams(vmem_limit_bytes=mib * MIB)


def cost(flops, nbytes):
    return pl.CostEstimate(flops=flops, bytes_accessed=nbytes, transcendentals=0)


def turn_kernel(at_ref, rows_ref, out_ref, wide_ref):
    step = pl.program_id(0)
    wide_ref[...] = rows_ref[...].T
    for side in range(2):
        source = pl.multiple_of(at_ref[8] + 2 * UNIT * side, 32)
        target = pl.multiple_of(at_ref[2 * step + side], 32)
        out_ref[pl.ds(target, UNIT)] = wide_ref[pl.ds(source, UNIT)]


def turn(at, rows):
    return pl.pallas_call(
        turn_kernel,
        grid_spec=pltpu.PrefetchScalarGridSpec(
            num_scalar_prefetch=1,
            grid=(4,),
            in_specs=[pl.BlockSpec((TOK, 4 * UNIT), lambda i, s: (0, i))],
            out_specs=pl.BlockSpec((HALF, TOK), lambda i, s: (0, 0)),
            scratch_shapes=[pltpu.VMEM((4 * UNIT, TOK), BF)],
        ),
        out_shape=jax.ShapeDtypeStruct((HALF, TOK), BF),
        compiler_params=params(14),
        cost_estimate=cost(0, 3 * TOK * D),
        name="turn",
    )(at, rows)


def back_kernel(rows_ref, out_ref):
    out_ref[...] = rows_ref[...].T


def back(turned):
    tile = 768
    return pl.pallas_call(
        back_kernel,
        grid=(HALF // tile,),
        in_specs=[pl.BlockSpec((tile, TOK), lambda i: (i, 0))],
        out_specs=pl.BlockSpec((TOK, tile), lambda i: (0, i)),
        out_shape=jax.ShapeDtypeStruct((TOK, HALF), BF),
        compiler_params=params(8),
        cost_estimate=cost(0, 4 * TOK * HALF),
        name="back",
    )(turned)


def dot(a, b):
    return jnp.dot(a, b, preferred_element_type=F32)


def first_kernel(rows_ref, *refs):
    out_ref, block = refs[4:]
    for i in range(4):
        block[UNIT * i : UNIT * i + UNIT] = refs[i][...]
    out_ref[...] = dot(rows_ref[...], block[...])


def second_kernel(rows_ref, even, odd, wide, acc_ref, out_ref, block):
    came = {EVEN: even, ODD: odd, WIDE: wide}
    for dim in (EVEN, ODD, WIDE):
        for i, (away, part) in enumerate(SENT[dim]):
            at = rows_of(away | dim, part).start - FIRST
            block[at : at + PART] = came[dim][PART * i : PART * i + PART]
    used = 3 * UNIT
    block[used:] = jnp.zeros((block.shape[0] - used, KVW), BF)
    out_ref[...] = acc_ref[...] + dot(rows_ref[:, : block.shape[0]], block[...])


def third_kernel(rows_ref, even, odd, wide, acc_ref, out_ref, block):
    came = {EVEN: even, ODD: odd, WIDE: wide}
    block[:PART] = jnp.zeros((PART, KVW), BF)
    for part in PARTS:
        block[PART * (part + 1) : PART * (part + 2)] = came[ORDERS[part][2]][...]
    total = acc_ref[...] + dot(rows_ref[...], block[...])
    out_ref[...] = (total * (1.0 / math.sqrt(D))).astype(BF)


def project(kernel, rows, width, index, weights, acc=None):
    last = kernel is third_kernel
    extra = [] if acc is None else [acc]
    whole = pl.BlockSpec((TOK, KVW), lambda i: (0, 0))
    depth = {first_kernel: FIRST, second_kernel: 7 * 128, third_kernel: QUAD}[kernel]
    return pl.pallas_call(
        kernel,
        grid=(1,),
        in_specs=[pl.BlockSpec((TOK, width), lambda i: (0, index))]
        + [pl.BlockSpec(value.shape, lambda i: (0, 0)) for value in weights]
        + [whole] * len(extra),
        out_specs=whole,
        out_shape=jax.ShapeDtypeStruct((TOK, KVW), BF if last else F32),
        scratch_shapes=[pltpu.VMEM((depth, KVW), BF)],
        compiler_params=params(17),
        cost_estimate=cost(2 * TOK * KVW * depth, 7 * MIB),
        name=kernel.__name__,
    )(rows, *weights, *extra)


def grad_blocks(groups, turned, residuals, dtype):
    def kernel(one, two, one_res, two_res, *outs):
        for group, out in zip(groups, outs):
            total = None
            for ref, res in ((one, one_res), (two, two_res)):
                rows = jnp.concatenate([ref[rows_of(*unit)] for unit in group], axis=0)
                term = dot(rows, res[...])
                total = term if total is None else total + term
            out[...] = total.astype(out.dtype)

    sizes = [PART * len(group) for group in groups]
    here = pl.BlockSpec(memory_space=pltpu.VMEM)
    return pl.pallas_call(
        kernel,
        in_specs=[here] * 4,
        out_specs=[here] * len(groups),
        out_shape=[jax.ShapeDtypeStruct((size, KVW), dtype) for size in sizes],
        compiler_params=params(14),
        cost_estimate=cost(4 * sum(sizes) * KVW * TOK, 5 * MIB),
        name="grad",
    )(*turned, *residuals)


def inner_kernel(*refs):
    stay, came = refs[0:3], refs[3:6]
    w_ref, m_ref, v_ref, g_ref, m_out, v_out, w_out, delta_out = refs[6:]
    tile = m_out.shape[1]
    columns = pl.ds(pl.multiple_of(pl.program_id(0) * tile, tile), tile)
    for part in PARTS:
        rows = slice(PART * part, PART * part + PART)
        grad = stay[part][:, columns] + came[part][:, columns].astype(F32)
        grad = grad * (1.0 / math.sqrt(TOK * 16))
        first = first_decay * m_ref[rows, columns] + (1.0 - first_decay) * grad
        second = second_decay * v_ref[rows, columns] + (1.0 - second_decay) * grad * grad
        m_out[rows] = first
        v_out[rows] = second
        wide = w_ref[rows, columns].astype(F32)
        weight = (
            wide - inner_rate * (first / (jnp.sqrt(second) + adam_eps) + weight_decay * wide)
        ).astype(BF)
        w_out[rows] = weight
        delta = (g_ref[rows, columns] - weight.astype(F32)).astype(BF)
        for group in range(delta_out.shape[0]):
            delta_out[group, rows] = delta[:, 128 * group : 128 * group + 128]


def inner(stay, came, weight, first, second, base):
    tile = 512
    here = pl.BlockSpec(memory_space=pltpu.VMEM)
    block = pl.BlockSpec((UNIT, tile), lambda i: (0, i))
    wide = jax.ShapeDtypeStruct((UNIT, KVW), F32)
    return pl.pallas_call(
        inner_kernel,
        grid=(KVW // tile,),
        in_specs=[here] * 10,
        out_specs=[block, block, block, pl.BlockSpec((tile // 128, UNIT, 128), lambda i: (i, 0, 0))],
        out_shape=[
            wide,
            wide,
            jax.ShapeDtypeStruct((UNIT, KVW), BF),
            jax.ShapeDtypeStruct((KVW // 128, UNIT, 128), BF),
        ],
        compiler_params=params(16),
        cost_estimate=cost(20 * UNIT * KVW, 9 * MIB),
        name="inner",
    )(*stay, *came, weight, first, second, base)


def total_kernel(parts_ref, out_ref):
    out_ref[...] = jnp.sum(parts_ref[...].astype(F32), axis=0).astype(BF)


def totals(parts):
    return pl.pallas_call(
        total_kernel,
        out_shape=jax.ShapeDtypeStruct(parts.shape[1:], BF),
        compiler_params=params(8),
        cost_estimate=cost(0, MIB),
        name="totals",
    )(parts)


def replica_mean(delta):
    pieces = lax.all_to_all(delta, "replica", 0, 0, axis_index_groups=ALONG_Z)
    part = totals(pieces)
    other = lax.ppermute(part, "replica", SWAP_LAST)
    mean = ((part.astype(F32) + other.astype(F32)) * (1.0 / REPLICAS)).astype(BF)
    pieces = jnp.broadcast_to(mean[None], pieces.shape)
    return lax.all_to_all(pieces, "replica", 0, 0, axis_index_groups=ALONG_Z)


def outer_kernel(mean_ref, w_ref, g_ref, o_ref, local_out, global_out, momentum_out):
    tile = local_out.shape[1]
    columns = pl.ds(pl.multiple_of(pl.program_id(0) * tile, tile), tile)
    first = pl.program_id(0) * (tile // 128)
    mean = jnp.concatenate([mean_ref[first + i] for i in range(tile // 128)], axis=1).astype(F32)
    momentum = outer_mu * o_ref[:, columns] + mean
    base = g_ref[:, columns] - outer_rate * (mean + outer_mu * momentum)
    momentum_out[...] = momentum
    global_out[...] = base
    mixed = mix_keep * w_ref[:, columns].astype(F32) + (1.0 - mix_keep) * base
    local_out[...] = mixed.astype(BF)


def outer(mean, weight, base, momentum):
    tile = 512
    here = pl.BlockSpec(memory_space=pltpu.VMEM)
    block = pl.BlockSpec((UNIT, tile), lambda i: (0, i))
    wide = jax.ShapeDtypeStruct((UNIT, KVW), F32)
    return pl.pallas_call(
        outer_kernel,
        grid=(KVW // tile,),
        in_specs=[here] * 4,
        out_specs=[block, block, block],
        out_shape=[jax.ShapeDtypeStruct((UNIT, KVW), BF), wide, wide],
        compiler_params=params(16),
        cost_estimate=cost(8 * UNIT * KVW, 7 * MIB),
        name="outer",
    )(mean, weight, base, momentum)


def local(
    tokens, targets, local_weights, first_moment, second_moment, global_weights, outer_momentum
):
    rows = tokens[0]
    wanted = targets[0]
    weight = local_weights[0]
    me = lax.axis_index("fsdp").astype(jnp.int32)
    places = []
    for chip in range(8):
        place = jnp.int32(0)
        for i, away in enumerate(ORDER):
            place = jnp.where((me >> 1) ^ chip_mask(away) == chip, UNIT * i, place)
        places.append(place)
    at = jnp.stack([*places, UNIT * (me & 1)]).astype(jnp.int32)
    at, weight, rows = lax.optimization_barrier((at, weight, rows))

    rows_other = swap(rows)
    dims = (EVEN, ODD, WIDE)
    near = {dim: flip(weight, dim) for dim in dims}
    kept = turn(at, rows)
    kept_rows = back(kept)
    (near, kept, kept_rows, rows_other) = lax.optimization_barrier(
        (near, kept, kept_rows, rows_other)
    )
    second = {
        dim: flip(
            jnp.concatenate(
                [near[away][PART * part : PART * part + PART] for away, part in SENT[dim]], axis=0
            ),
            dim,
        )
        for dim in dims
    }
    wanted_other = swap(wanted)
    received = turn(at, rows_other)
    received_rows = back(received)
    first_weights = [weight, *(near[dim] for dim in dims)]
    sum_kept = project(first_kernel, kept_rows, FIRST, 0, first_weights)
    sum_received = project(first_kernel, received_rows, FIRST, 0, first_weights)
    second, sum_kept, sum_received = lax.optimization_barrier((second, sum_kept, sum_received))
    third = {}
    for part in PARTS:
        one, two, three = ORDERS[part]
        index = SENT[two].index((one, part))
        third[three] = flip(second[two][PART * index : PART * index + PART], three)
    second_weights = [second[dim] for dim in dims]
    sum_received = project(second_kernel, received_rows, FIRST, 1, second_weights, sum_received)
    sum_kept = project(second_kernel, kept_rows, FIRST, 1, second_weights, sum_kept)
    third, sum_kept, sum_received, wanted_other = lax.optimization_barrier(
        (third, sum_kept, sum_received, wanted_other)
    )
    turned = (kept, received)
    third_weights = [third[dim] for dim in dims]
    own_received = project(third_kernel, received_rows, QUAD, 5, third_weights, sum_received)
    cross_kept = swap(own_received)
    own_kept = project(third_kernel, kept_rows, QUAD, 5, third_weights, sum_kept)
    cross_received = swap(own_kept)
    residuals = (
        (own_kept.astype(F32) + cross_kept.astype(F32) - wanted.astype(F32)).astype(BF),
        (own_received.astype(F32) + cross_received.astype(F32) - wanted_other.astype(F32)).astype(
            BF
        ),
    )

    pass_on, keep = [], []
    for part in PARTS:
        one, two, three = ORDERS[part]
        pass_on.append([(two, part), (one | two, part)])
        keep.append([(0, part), (one, part)])

    def beyond(group, part):
        return [(away | ORDERS[part][2], part) for away, _ in group]

    (quad,) = grad_blocks(
        [beyond(pass_on[0], 0) + beyond(keep[0], 0)], turned, residuals, BF
    )
    quad = flip(quad, ORDERS[0][2])
    came, late = [], []
    for part in (1, 2):
        go, stay = grad_blocks(
            [beyond(pass_on[part], part), beyond(keep[part], part)], turned, residuals, BF
        )
        came.append(flip(go, ORDERS[part][2]))
        late.append(stay)
    late = [flip(late[part - 1], ORDERS[part][2]) for part in (1, 2)]
    came = [quad[:PAIR], *came]
    late = [quad[PAIR:], *late]
    sums = grad_blocks(pass_on, turned, residuals, F32)
    sent = [(sums[part] + came[part].astype(F32)).astype(BF) for part in PARTS]
    came = [flip(sent[part], ORDERS[part][1]) for part in PARTS]
    late, residuals = lax.optimization_barrier((late, residuals))
    sums = grad_blocks(keep, turned, residuals, F32)
    sums = [sums[part] + late[part].astype(F32) + came[part].astype(F32) for part in PARTS]
    came = [flip(sums[part][PART:].astype(BF), ORDERS[part][0]) for part in PARTS]
    sums = [sums[part][:PART] for part in PARTS]

    first, second, weight, delta = inner(
        sums, came, weight, first_moment[0], second_moment[0], global_weights
    )
    mean = replica_mean(delta)
    new_local, new_global, new_momentum = outer(mean, weight, global_weights, outer_momentum)
    return (new_local[None], first[None], second[None], new_global, new_momentum)


def solution(mesh):
    return jax.shard_map(
        local,
        mesh=mesh,
        in_specs=(
            P("replica", "fsdp", None),
            P("replica", "fsdp", None),
            P("replica", "fsdp", None),
            P("replica", "fsdp", None),
            P("replica", "fsdp", None),
            P("fsdp", None),
            P("fsdp", None),
        ),
        out_specs=(
            P("replica", "fsdp", None),
            P("replica", "fsdp", None),
            P("replica", "fsdp", None),
            P("fsdp", None),
            P("fsdp", None),
        ),
        check_vma=False,
    )
```

time: 155 us -> 149 us (0.961)
  starting transfers between devices: 31.8 us -> 38.7 us
  blocking collectives: 41.9 us -> 37.9 us
  waiting for transfers between devices: 44.3 us -> 40.3 us
  Pallas kernels: 27.6 us -> 23.9 us
  other arithmetic: 4.23 us -> 2.25 us
    ppermute x18 -> x20, starting transfers between devices: 30.3 us -> 36.2 us  [flip(): lax.ppermute(value, 'fsdp', [(i, i ^ 2 * CHIP_FLIP[dim]) for i in range(1...]
    pallas_call x16 -> x17, Pallas kernels: 27.5 us -> 23.8 us  [the longest x6 7.03 us: project(): pl.pallas_call(kernel, grid=(1,), in_specs=[pl.BlockSpec((TOK, width), la...]
    ppermute x18 -> x20, waiting for transfers between devices: 39 us -> 35.3 us  [flip(): lax.ppermute(value, 'fsdp', [(i, i ^ 2 * CHIP_FLIP[dim]) for i in range(1...]
    all_to_all x1, blocking collectives: 24.8 us -> 21.6 us  [replica_mean(): pieces = lax.all_to_all(delta, 'replica', 0, 0, axis_index_groups=ALONG_Z)]
  transfers between devices with their start and end apart: 23 -> 25, of which waited for: 18 -> 18; matrix products, arithmetic and copies ran while one was open for 3% -> 1% of each run, Pallas kernels for 12% -> 12%
where the time goes in v3:
time: 149 us; the launch traced here: 147 us
  waiting for transfers between devices  40.3 us (27%)
  starting transfers between devices  38.7 us (26%)
  blocking collectives  37.9 us (25%)
  Pallas kernels  23.9 us (16%)
  local copies, waits for them, and re-layouts  2.91 us (2%)
  other arithmetic  2.25 us (2%)
    ppermute x20, starting transfers between devices, flip(): lax.ppermute(value, 'fsdp', [(i, i ^ 2 * CHIP_FLIP[dim]) for i in range(1...  36.2 us
    ppermute x20, waiting for transfers between devices, flip(): lax.ppermute(value, 'fsdp', [(i, i ^ 2 * CHIP_FLIP[dim]) for i in range(1...  35.3 us
    all_to_all x1, blocking collectives, replica_mean(): pieces = lax.all_to_all(delta, 'replica', 0, 0, axis_index_groups=ALONG_Z)  21.6 us
    all_to_all x1, blocking collectives, replica_mean(): return lax.all_to_all(pieces, 'replica', 0, 0, axis_index_groups=ALONG_Z)  16.4 us
    pallas_call x6, Pallas kernels, project(): pl.pallas_call(kernel, grid=(1,), in_specs=[pl.BlockSpec((TOK, width), la...  7.03 us
    pallas_call x5, Pallas kernels, grad_blocks(): pl.pallas_call(kernel, in_specs=[here] * 4, out_specs=[here] * len(groups...  5.75 us
    pallas_call x2, Pallas kernels, turn(): pl.pallas_call(turn_kernel, grid_spec=pltpu.PrefetchScalarGridSpec(num_sc...  5.13 us
  transfers between devices with their start and end apart: 25, of which 18 were waited for; matrix products, arithmetic and copies ran while one was open for 1% of the time, Pallas kernels for 12%

profile of v3, /device:TPU:2, one launch (start us, length us, event | category | flops | bytes accessed | tf_op | source)
XLA Modules:
  0.0 147.4 jit_solution(17829616928974838574)
XLA Ops:
  1.1 2.4 %collective-permute-start = (bf16[288,1024]{1,0:T(8,128)(2,1)}, bf16[288,1024]{1,0:T(8,128)(2,1)S(1)}, u32[]{:S(2)}, u32[]{:S(2)}) collective-permute-start(bf16[288,1024]{1,0:T(8,128)(2,1)} %bitcast.18), channel_id=1, source_target_pairs={{0,2},{1,3},{2,0},{3,1},{4,6},{5,7},{6,4},{7,5},{8,10},{9,11},{10,... | collective-permute-start | bytes 1769480 | tf_op jit(solution)/shard_map/ppermute | solution.py:63
  3.9 3.2 %collective-permute-start.2 = (bf16[288,1024]{1,0:T(8,128)(2,1)}, bf16[288,1024]{1,0:T(8,128)(2,1)S(1)}, u32[]{:S(2)}, u32[]{:S(2)}) collective-permute-start(bf16[288,1024]{1,0:T(8,128)(2,1)} %bitcast.20), channel_id=1, source_target_pairs={{0,8},{1,9},{2,10},{3,11},{4,12},{5,13},{6,14},{7,15},{8,0},{9,1},... | collective-permute-start | bytes 1769480 | tf_op jit(solution)/shard_map/ppermute | solution.py:63
  7.1 2.3 %copy-done.1 = bf16[1,512,4608]{2,1,0:T(8,128)(2,1)S(1)} copy-done((bf16[1,512,4608]{2,1,0:T(8,128)(2,1)S(1)}, bf16[1,512,4608]{2,1,0:T(8,128)(2,1)}, u32[]{:S(2)}) %copy-start.1) | copy-done | bytes 4718616
  9.4 2.6 %turn.2.rows_ref.one = bf16[2304,512]{1,0:T(8,128)(2,1)S(1)} custom-call(s32[9]{0:T(128)S(1)} %stack.39.at_ref, bf16[512,4608]{1,0:T(8,128)(2,1)S(1)} %bitcast.25), custom_call_target="tpu_custom_call" | custom-call | bytes 7077888 | tf_op jit(solution)/shard_map/turn/pallas_call | solution.py:88
  12.9 4.6 %collective-permute-done.refs_1_ = bf16[288,1024]{1,0:T(8,128)(2,1)S(1)} collective-permute-done((bf16[288,1024]{1,0:T(8,128)(2,1)}, bf16[288,1024]{1,0:T(8,128)(2,1)S(1)}, u32[]{:S(2)}, u32[]{:S(2)}) %collective-permute-start) | collective-permute-done | bytes 589856 | tf_op jit(solution)/shard_map/ppermute | solution.py:63
  23.5 2.7 %collective-permute-start.6 = (bf16[288,1024]{1,0:T(8,128)(2,1)S(1)}, bf16[288,1024]{1,0:T(8,128)(2,1)S(1)}, u32[]{:S(2)}, u32[]{:S(2)}) collective-permute-start(bf16[288,1024]{1,0:T(8,128)(2,1)S(1)} %get-tuple-element.95), channel_id=1, source_target_pairs={{0,8},{1,9},{2,10},{3,11},{4,12},{5,13},{6,14},{7,15},{8,0},{9,1},... | collective-permute-start | bytes 1769480 | tf_op jit(solution)/shard_map/ppermute | solution.py:63
  26.2 2.6 %turn.3.rows_ref.two = bf16[2304,512]{1,0:T(8,128)(2,1)S(1)} custom-call(s32[9]{0:T(128)S(1)} %stack.39.at_ref, bf16[512,4608]{1,0:T(8,128)(2,1)S(1)} %collective-permute-done.3.rows_ref), custom_call_target="tpu_custom_call" | custom-call | bytes 7077888 | tf_op jit(solution)/shard_map/turn/pallas_call | solution.py:88
  32.9 2.4 %collective-permute-done.4.even = bf16[288,1024]{1,0:T(8,128)(2,1)S(1)} collective-permute-done((bf16[288,1024]{1,0:T(8,128)(2,1)S(1)}, bf16[288,1024]{1,0:T(8,128)(2,1)S(1)}, u32[]{:S(2)}, u32[]{:S(2)}) %collective-permute-start.4) | collective-permute-done | bytes 589856 | tf_op jit(solution)/shard_map/ppermute | solution.py:63
  36.5 2.4 %collective-permute-done.6.wide = bf16[288,1024]{1,0:T(8,128)(2,1)S(1)} collective-permute-done((bf16[288,1024]{1,0:T(8,128)(2,1)S(1)}, bf16[288,1024]{1,0:T(8,128)(2,1)S(1)}, u32[]{:S(2)}, u32[]{:S(2)}) %collective-permute-start.6) | collective-permute-done | bytes 589856 | tf_op jit(solution)/shard_map/ppermute | solution.py:63
  41.2 3.2 %collective-permute-start.9 = (bf16[96,1024]{1,0:T(8,128)(2,1)S(1)}, bf16[96,1024]{1,0:T(8,128)(2,1)S(1)}, u32[]{:S(2)}, u32[]{:S(2)}) collective-permute-start(bf16[96,1024]{1,0:T(8,128)(2,1)S(1)} %slice.65), channel_id=1, source_target_pairs={{0,8},{1,9},{2,10},{3,11},{4,12},{5,13},{6,14},{7,15},{8,0},{9,1},... | collective-permute-start | bytes 589832 | tf_op jit(solution)/shard_map/ppermute | solution.py:63
  60.6 2.6 %collective-permute-start.17 = (bf16[192,1024]{1,0:T(8,128)(2,1)S(1)}, bf16[192,1024]{1,0:T(8,128)(2,1)S(1)}, u32[]{:S(2)}, u32[]{:S(2)}) collective-permute-start(bf16[192,1024]{1,0:T(8,128)(2,1)S(1)} %get-tuple-element.77), channel_id=1, source_target_pairs={{0,8},{1,9},{2,10},{3,11},{4,12},{5,13},{6,14},{7,15},{8,0},{9,1},... | collective-permute-start | bytes 1179656 | tf_op jit(solution)/shard_map/ppermute | solution.py:63
  67.4 2.7 %collective-permute-start.20 = (bf16[192,1024]{1,0:T(8,128)(2,1)S(1)}, bf16[192,1024]{1,0:T(8,128)(2,1)S(1)}, u32[]{:S(2)}, u32[]{:S(2)}) collective-permute-start(bf16[192,1024]{1,0:T(8,128)(2,1)S(1)} %add_convert_fusion), channel_id=1, source_target_pairs={{0,2},{1,3},{2,0},{3,1},{4,6},{5,7},{6,4},{7,5},{8,10},{9,11},{10,... | collective-permute-start | bytes 1179656 | tf_op jit(solution)/shard_map/ppermute | solution.py:63
  70.1 4.1 %collective-permute-done.17 = bf16[192,1024]{1,0:T(8,128)(2,1)S(1)} collective-permute-done((bf16[192,1024]{1,0:T(8,128)(2,1)S(1)}, bf16[192,1024]{1,0:T(8,128)(2,1)S(1)}, u32[]{:S(2)}, u32[]{:S(2)}) %collective-permute-start.17) | collective-permute-done | bytes 393248 | tf_op jit(solution)/shard_map/ppermute | solution.py:63
  75.3 3.1 %collective-permute-done.13 = bf16[384,1024]{1,0:T(8,128)(2,1)S(1)} collective-permute-done((bf16[384,1024]{1,0:T(8,128)(2,1)S(1)}, bf16[384,1024]{1,0:T(8,128)(2,1)S(1)}, u32[]{:S(2)}, u32[]{:S(2)}) %collective-permute-start.13) | collective-permute-done | bytes 786464 | tf_op jit(solution)/shard_map/ppermute | solution.py:63
  78.4 2.8 %collective-permute-done.14 = bf16[192,1024]{1,0:T(8,128)(2,1)S(1)} collective-permute-done((bf16[192,1024]{1,0:T(8,128)(2,1)S(1)}, bf16[192,1024]{1,0:T(8,128)(2,1)S(1)}, u32[]{:S(2)}, u32[]{:S(2)}) %collective-permute-start.14) | collective-permute-done | bytes 393248 | tf_op jit(solution)/shard_map/ppermute | solution.py:63
  81.4 2.6 %collective-permute-start.16 = (bf16[192,1024]{1,0:T(8,128)(2,1)S(1)}, bf16[192,1024]{1,0:T(8,128)(2,1)S(1)}, u32[]{:S(2)}, u32[]{:S(2)}) collective-permute-start(bf16[192,1024]{1,0:T(8,128)(2,1)S(1)} %add_convert_fusion.2), channel_id=1, source_target_pairs={{0,8},{1,9},{2,10},{3,11},{4,12},{5,13},{6,14},{7,15},{8,0},{9,1},... | collective-permute-start | bytes 1179656 | tf_op jit(solution)/shard_map/ppermute | solution.py:63
  85.9 2.7 %collective-permute-start.23 = (bf16[96,1024]{1,0:T(8,128)(2,1)S(1)}, bf16[96,1024]{1,0:T(8,128)(2,1)S(1)}, u32[]{:S(2)}, u32[]{:S(2)}) collective-permute-start(bf16[96,1024]{1,0:T(8,128)(2,1)S(1)} %slice.86), channel_id=1, source_target_pairs={{0,8},{1,9},{2,10},{3,11},{4,12},{5,13},{6,14},{7,15},{8,0},{9,1},... | collective-permute-start | bytes 589832 | tf_op jit(solution)/shard_map/ppermute | solution.py:63
  88.8 1.8 %collective-permute-start.22 = (bf16[96,1024]{1,0:T(8,128)(2,1)S(1)}, bf16[96,1024]{1,0:T(8,128)(2,1)S(1)}, u32[]{:S(2)}, u32[]{:S(2)}) collective-permute-start(bf16[96,1024]{1,0:T(8,128)(2,1)S(1)} %slice.87), channel_id=1, source_target_pairs={{0,2},{1,3},{2,0},{3,1},{4,6},{5,7},{6,4},{7,5},{8,10},{9,11},{10,... | collective-permute-start | bytes 589832 | tf_op jit(solution)/shard_map/ppermute | solution.py:63
  90.7 4.1 %collective-permute-done.16 = bf16[192,1024]{1,0:T(8,128)(2,1)S(1)} collective-permute-done((bf16[192,1024]{1,0:T(8,128)(2,1)S(1)}, bf16[192,1024]{1,0:T(8,128)(2,1)S(1)}, u32[]{:S(2)}, u32[]{:S(2)}) %collective-permute-start.16) | collective-permute-done | bytes 393248 | tf_op jit(solution)/shard_map/ppermute | solution.py:63
  96.9 3.9 %collective-permute-done.21.refs_3_ = bf16[96,1024]{1,0:T(8,128)(2,1)S(1)} collective-permute-done((bf16[96,1024]{1,0:T(8,128)(2,1)S(1)}, bf16[96,1024]{1,0:T(8,128)(2,1)S(1)}, u32[]{:S(2)}, u32[]{:S(2)}) %collective-permute-start.21) | collective-permute-done | bytes 196640 | tf_op jit(solution)/shard_map/ppermute | solution.py:63
  100.8 2.2 %inner.1 = (f32[288,1024]{1,0:T(8,128)}, f32[288,1024]{1,0:T(8,128)}, bf16[288,1024]{1,0:T(8,128)(2,1)S(1)}, bf16[8,288,128]{2,1,0:T(8,128)(2,1)S(1)}) custom-call(f32[96,1024]{1,0:T(8,128)S(1)} %slice.76.refs_0_, f32[96,1024]{1,0:T(8,128)S(1)} %slice.77.refs_1_, f32[96,1024]{1,0:T(8,128)S(1)} %slice.78.refs_2_, ...), custom_call_target="tpu_custom_call" | custom-call | flops 5898240 | bytes 9437184 | tf_op jit(solution)/shard_map/inner/pallas_call | solution.py:224
  103.0 21.6 %all_to_all.10.parts_ref = bf16[8,288,128]{2,1,0:T(8,128)(2,1)S(1)} all-to-all(bf16[8,288,128]{2,1,0:T(8,128)(2,1)S(1)} %get-tuple-element.82), channel_id=1, replica_groups={{0,32,64,96,128,160,192,224},{16,48,80,112,144,176,208,240},{1,33,65,97..., dimensions={0} | all-to-all | bytes 1179648 | tf_op jit(solution)/shard_map/all_to_all | solution.py:256
  126.3 2.8 %collective-permute-done.24 = bf16[288,128]{1,0:T(8,128)(2,1)S(1)} collective-permute-done((bf16[288,128]{1,0:T(8,128)(2,1)S(1)}, bf16[288,128]{1,0:T(8,128)(2,1)S(1)}, u32[]{:S(2)}, u32[]{:S(2)}) %collective-permute-start.24) | collective-permute-done | bytes 73760 | tf_op jit(solution)/shard_map/ppermute | solution.py:258
  129.2 16.4 %all_to_all.11.mean_ref = bf16[8,288,128]{2,1,0:T(8,128)(2,1)S(1)} all-to-all(bf16[8,288,128]{2,1,0:T(8,128)(2,1)S(1)} %broadcast_in_dim.15), channel_id=1, replica_groups={{0,32,64,96,128,160,192,224},{16,48,80,112,144,176,208,240},{1,33,65,97..., dimensions={0} | all-to-all | bytes 1179648 | tf_op jit(solution)/shard_map/all_to_all | solution.py:261
  (87 shorter events, 44.1 us)
Async XLA Ops:
  1.0 19.7 %collective-permute-start.3 = (bf16[512,4608]{1,0:T(8,128)(2,1)}, bf16[512,4608]{1,0:T(8,128)(2,1)S(1)}, u32[]{:S(2)}, u32[]{:S(2)}) collective-permute-start(bf16[512,4608]{1,0:T(8,128)(2,1)} %bitcast.24), channel_id=1, source_target_pairs={{0,1},{1,0},{2,3},{3,2},{4,5},{5,4},{6,7},{7,6},{8,9},{9,8},{10,11... | collective-permute-start | bytes 14155784 | tf_op jit(solution)/shard_map/ppermute | solution.py:67
  1.1 16.5 %collective-permute-start = (bf16[288,1024]{1,0:T(8,128)(2,1)}, bf16[288,1024]{1,0:T(8,128)(2,1)S(1)}, u32[]{:S(2)}, u32[]{:S(2)}) collective-permute-start(bf16[288,1024]{1,0:T(8,128)(2,1)} %bitcast.18), channel_id=1, source_target_pairs={{0,2},{1,3},{2,0},{3,1},{4,6},{5,7},{6,4},{7,5},{8,10},{9,11},{10,... | collective-permute-start | bytes 1769480 | tf_op jit(solution)/shard_map/ppermute | solution.py:63
  3.4 15.6 %collective-permute-start.1 = (bf16[288,1024]{1,0:T(8,128)(2,1)}, bf16[288,1024]{1,0:T(8,128)(2,1)S(1)}, u32[]{:S(2)}, u32[]{:S(2)}) collective-permute-start(bf16[288,1024]{1,0:T(8,128)(2,1)} %bitcast.19), channel_id=1, source_target_pairs={{0,6},{1,7},{2,4},{3,5},{4,2},{5,3},{6,0},{7,1},{8,14},{9,15},{10,... | collective-permute-start | bytes 1769480 | tf_op jit(solution)/shard_map/ppermute | solution.py:63
  3.9 16.8 %collective-permute-start.2 = (bf16[288,1024]{1,0:T(8,128)(2,1)}, bf16[288,1024]{1,0:T(8,128)(2,1)S(1)}, u32[]{:S(2)}, u32[]{:S(2)}) collective-permute-start(bf16[288,1024]{1,0:T(8,128)(2,1)} %bitcast.20), channel_id=1, source_target_pairs={{0,8},{1,9},{2,10},{3,11},{4,12},{5,13},{6,14},{7,15},{8,0},{9,1},... | collective-permute-start | bytes 1769480 | tf_op jit(solution)/shard_map/ppermute | solution.py:63
  7.1 39.9 %collective-permute-start.10 = (bf16[512,1024]{1,0:T(8,128)(2,1)}, bf16[512,1024]{1,0:T(8,128)(2,1)S(1)}, u32[]{:S(2)}, u32[]{:S(2)}) collective-permute-start(bf16[512,1024]{1,0:T(8,128)(2,1)} %bitcast.28), channel_id=1, source_target_pairs={{0,1},{1,0},{2,3},{3,2},{4,5},{5,4},{6,7},{7,6},{8,9},{9,8},{10,11... | collective-permute-start | bytes 3145736 | tf_op jit(solution)/shard_map/ppermute | solution.py:67
  21.0 14.3 %collective-permute-start.4 = (bf16[288,1024]{1,0:T(8,128)(2,1)S(1)}, bf16[288,1024]{1,0:T(8,128)(2,1)S(1)}, u32[]{:S(2)}, u32[]{:S(2)}) collective-permute-start(bf16[288,1024]{1,0:T(8,128)(2,1)S(1)} %get-tuple-element.97), channel_id=1, source_target_pairs={{0,2},{1,3},{2,0},{3,1},{4,6},{5,7},{6,4},{7,5},{8,10},{9,11},{10,... | collective-permute-start | bytes 1769480 | tf_op jit(solution)/shard_map/ppermute | solution.py:63
  22.5 14.0 %collective-permute-start.5 = (bf16[288,1024]{1,0:T(8,128)(2,1)S(1)}, bf16[288,1024]{1,0:T(8,128)(2,1)S(1)}, u32[]{:S(2)}, u32[]{:S(2)}) collective-permute-start(bf16[288,1024]{1,0:T(8,128)(2,1)S(1)} %get-tuple-element.96), channel_id=1, source_target_pairs={{0,6},{1,7},{2,4},{3,5},{4,2},{5,3},{6,0},{7,1},{8,14},{9,15},{10,... | collective-permute-start | bytes 1769480 | tf_op jit(solution)/shard_map/ppermute | solution.py:63
  23.5 15.4 %collective-permute-start.6 = (bf16[288,1024]{1,0:T(8,128)(2,1)S(1)}, bf16[288,1024]{1,0:T(8,128)(2,1)S(1)}, u32[]{:S(2)}, u32[]{:S(2)}) collective-permute-start(bf16[288,1024]{1,0:T(8,128)(2,1)S(1)} %get-tuple-element.95), channel_id=1, source_target_pairs={{0,8},{1,9},{2,10},{3,11},{4,12},{5,13},{6,14},{7,15},{8,0},{9,1},... | collective-permute-start | bytes 1769480 | tf_op jit(solution)/shard_map/ppermute | solution.py:63
  38.9 8.1 %collective-permute-start.7 = (bf16[96,1024]{1,0:T(8,128)(2,1)S(1)}, bf16[96,1024]{1,0:T(8,128)(2,1)S(1)}, u32[]{:S(2)}, u32[]{:S(2)}) collective-permute-start(bf16[96,1024]{1,0:T(8,128)(2,1)S(1)} %slice.63), channel_id=1, source_target_pairs={{0,2},{1,3},{2,0},{3,1},{4,6},{5,7},{6,4},{7,5},{8,10},{9,11},{10,... | collective-permute-start | bytes 589832 | tf_op jit(solution)/shard_map/ppermute | solution.py:63
  40.6 6.4 %collective-permute-start.8 = (bf16[96,1024]{1,0:T(8,128)(2,1)S(1)}, bf16[96,1024]{1,0:T(8,128)(2,1)S(1)}, u32[]{:S(2)}, u32[]{:S(2)}) collective-permute-start(bf16[96,1024]{1,0:T(8,128)(2,1)S(1)} %slice.64), channel_id=1, source_target_pairs={{0,6},{1,7},{2,4},{3,5},{4,2},{5,3},{6,0},{7,1},{8,14},{9,15},{10,... | collective-permute-start | bytes 589832 | tf_op jit(solution)/shard_map/ppermute | solution.py:63
  41.2 7.3 %collective-permute-start.9 = (bf16[96,1024]{1,0:T(8,128)(2,1)S(1)}, bf16[96,1024]{1,0:T(8,128)(2,1)S(1)}, u32[]{:S(2)}, u32[]{:S(2)}) collective-permute-start(bf16[96,1024]{1,0:T(8,128)(2,1)S(1)} %slice.65), channel_id=1, source_target_pairs={{0,8},{1,9},{2,10},{3,11},{4,12},{5,13},{6,14},{7,15},{8,0},{9,1},... | collective-permute-start | bytes 589832 | tf_op jit(solution)/shard_map/ppermute | solution.py:63
  50.2 3.4 %collective-permute-start.12 = (bf16[512,1024]{1,0:T(8,128)(2,1)S(1)}, bf16[512,1024]{1,0:T(8,128)(2,1)S(1)}, u32[]{:S(2)}, u32[]{:S(2)}) collective-permute-start(bf16[512,1024]{1,0:T(8,128)(2,1)S(1)} %third_kernel.2), channel_id=1, source_target_pairs={{0,1},{1,0},{2,3},{3,2},{4,5},{5,4},{6,7},{7,6},{8,9},{9,8},{10,11... | collective-permute-start | bytes 3145736 | tf_op jit(solution)/shard_map/ppermute | solution.py:67
  55.3 12.0 %collective-permute-start.19 = (bf16[192,1024]{1,0:T(8,128)(2,1)S(1)}, bf16[192,1024]{1,0:T(8,128)(2,1)S(1)}, u32[]{:S(2)}, u32[]{:S(2)}) collective-permute-start(bf16[192,1024]{1,0:T(8,128)(2,1)S(1)} %get-tuple-element.81), channel_id=1, source_target_pairs={{0,6},{1,7},{2,4},{3,5},{4,2},{5,3},{6,0},{7,1},{8,14},{9,15},{10,... | collective-permute-start | bytes 1179656 | tf_op jit(solution)/shard_map/ppermute | solution.py:63
  57.9 20.5 %collective-permute-start.13 = (bf16[384,1024]{1,0:T(8,128)(2,1)S(1)}, bf16[384,1024]{1,0:T(8,128)(2,1)S(1)}, u32[]{:S(2)}, u32[]{:S(2)}) collective-permute-start(bf16[384,1024]{1,0:T(8,128)(2,1)S(1)} %grad.5), channel_id=1, source_target_pairs={{0,2},{1,3},{2,0},{3,1},{4,6},{5,7},{6,4},{7,5},{8,10},{9,11},{10,... | collective-permute-start | bytes 2359304 | tf_op jit(solution)/shard_map/ppermute | solution.py:63
  60.6 13.6 %collective-permute-start.17 = (bf16[192,1024]{1,0:T(8,128)(2,1)S(1)}, bf16[192,1024]{1,0:T(8,128)(2,1)S(1)}, u32[]{:S(2)}, u32[]{:S(2)}) collective-permute-start(bf16[192,1024]{1,0:T(8,128)(2,1)S(1)} %get-tuple-element.77), channel_id=1, source_target_pairs={{0,8},{1,9},{2,10},{3,11},{4,12},{5,13},{6,14},{7,15},{8,0},{9,1},... | collective-permute-start | bytes 1179656 | tf_op jit(solution)/shard_map/ppermute | solution.py:63
  63.2 15.2 %collective-permute-start.15 = (bf16[192,1024]{1,0:T(8,128)(2,1)S(1)}, bf16[192,1024]{1,0:T(8,128)(2,1)S(1)}, u32[]{:S(2)}, u32[]{:S(2)}) collective-permute-start(bf16[192,1024]{1,0:T(8,128)(2,1)S(1)} %get-tuple-element.68), channel_id=1, source_target_pairs={{0,6},{1,7},{2,4},{3,5},{4,2},{5,3},{6,0},{7,1},{8,14},{9,15},{10,... | collective-permute-start | bytes 1179656 | tf_op jit(solution)/shard_map/ppermute | solution.py:63
  64.7 16.5 %collective-permute-start.14 = (bf16[192,1024]{1,0:T(8,128)(2,1)S(1)}, bf16[192,1024]{1,0:T(8,128)(2,1)S(1)}, u32[]{:S(2)}, u32[]{:S(2)}) collective-permute-start(bf16[192,1024]{1,0:T(8,128)(2,1)S(1)} %get-tuple-element.67), channel_id=1, source_target_pairs={{0,8},{1,9},{2,10},{3,11},{4,12},{5,13},{6,14},{7,15},{8,0},{9,1},... | collective-permute-start | bytes 1179656 | tf_op jit(solution)/shard_map/ppermute | solution.py:63
  67.4 18.3 %collective-permute-start.20 = (bf16[192,1024]{1,0:T(8,128)(2,1)S(1)}, bf16[192,1024]{1,0:T(8,128)(2,1)S(1)}, u32[]{:S(2)}, u32[]{:S(2)}) collective-permute-start(bf16[192,1024]{1,0:T(8,128)(2,1)S(1)} %add_convert_fusion), channel_id=1, source_target_pairs={{0,2},{1,3},{2,0},{3,1},{4,6},{5,7},{6,4},{7,5},{8,10},{9,11},{10,... | collective-permute-start | bytes 1179656 | tf_op jit(solution)/shard_map/ppermute | solution.py:63
  74.4 14.3 %collective-permute-start.18 = (bf16[192,1024]{1,0:T(8,128)(2,1)S(1)}, bf16[192,1024]{1,0:T(8,128)(2,1)S(1)}, u32[]{:S(2)}, u32[]{:S(2)}) collective-permute-start(bf16[192,1024]{1,0:T(8,128)(2,1)S(1)} %add_convert_fusion.1), channel_id=1, source_target_pairs={{0,6},{1,7},{2,4},{3,5},{4,2},{5,3},{6,0},{7,1},{8,14},{9,15},{10,... | collective-permute-start | bytes 1179656 | tf_op jit(solution)/shard_map/ppermute | solution.py:63
  81.4 13.4 %collective-permute-start.16 = (bf16[192,1024]{1,0:T(8,128)(2,1)S(1)}, bf16[192,1024]{1,0:T(8,128)(2,1)S(1)}, u32[]{:S(2)}, u32[]{:S(2)}) collective-permute-start(bf16[192,1024]{1,0:T(8,128)(2,1)S(1)} %add_convert_fusion.2), channel_id=1, source_target_pairs={{0,8},{1,9},{2,10},{3,11},{4,12},{5,13},{6,14},{7,15},{8,0},{9,1},... | collective-permute-start | bytes 1179656 | tf_op jit(solution)/shard_map/ppermute | solution.py:63
  85.9 11.0 %collective-permute-start.23 = (bf16[96,1024]{1,0:T(8,128)(2,1)S(1)}, bf16[96,1024]{1,0:T(8,128)(2,1)S(1)}, u32[]{:S(2)}, u32[]{:S(2)}) collective-permute-start(bf16[96,1024]{1,0:T(8,128)(2,1)S(1)} %slice.86), channel_id=1, source_target_pairs={{0,8},{1,9},{2,10},{3,11},{4,12},{5,13},{6,14},{7,15},{8,0},{9,1},... | collective-permute-start | bytes 589832 | tf_op jit(solution)/shard_map/ppermute | solution.py:63
  88.8 8.0 %collective-permute-start.22 = (bf16[96,1024]{1,0:T(8,128)(2,1)S(1)}, bf16[96,1024]{1,0:T(8,128)(2,1)S(1)}, u32[]{:S(2)}, u32[]{:S(2)}) collective-permute-start(bf16[96,1024]{1,0:T(8,128)(2,1)S(1)} %slice.87), channel_id=1, source_target_pairs={{0,2},{1,3},{2,0},{3,1},{4,6},{5,7},{6,4},{7,5},{8,10},{9,11},{10,... | collective-permute-start | bytes 589832 | tf_op jit(solution)/shard_map/ppermute | solution.py:63
  95.0 5.8 %collective-permute-start.21 = (bf16[96,1024]{1,0:T(8,128)(2,1)S(1)}, bf16[96,1024]{1,0:T(8,128)(2,1)S(1)}, u32[]{:S(2)}, u32[]{:S(2)}) collective-permute-start(bf16[96,1024]{1,0:T(8,128)(2,1)S(1)} %slice.88), channel_id=1, source_target_pairs={{0,6},{1,7},{2,4},{3,5},{4,2},{5,3},{6,0},{7,1},{8,14},{9,15},{10,... | collective-permute-start | bytes 589832 | tf_op jit(solution)/shard_map/ppermute | solution.py:63
  124.6 4.4 %collective-permute-start.24 = (bf16[288,128]{1,0:T(8,128)(2,1)S(1)}, bf16[288,128]{1,0:T(8,128)(2,1)S(1)}, u32[]{:S(2)}, u32[]{:S(2)}) collective-permute-start(bf16[288,128]{1,0:T(8,128)(2,1)S(1)} %totals.1), channel_id=1, source_target_pairs={{0,16},{16,0},{32,48},{48,32},{64,80},{80,64},{96,112},{112,96},{1... | collective-permute-start | bytes 221192 | tf_op jit(solution)/shard_map/ppermute | solution.py:258
  (10 other events, 56.8 us)

commit v4 on v3

--- a/solution.py
+++ b/solution.py
@@ -27,20 +27,20 @@
 REPLICAS = 16
 MIB = 1024 * 1024
 
-EVEN, ODD, WIDE = 1, 2, 4
-ORDER = (0, EVEN, ODD, WIDE, EVEN | ODD, ODD | WIDE, EVEN | WIDE, EVEN | ODD | WIDE)
-CHIP_FLIP = {EVEN: 1, ODD: 3, WIDE: 4}
+WIDE, EVEN, ODD = 1, 2, 4
+ORDER = (0, WIDE, EVEN, ODD, EVEN | ODD, ODD | WIDE, EVEN | WIDE, EVEN | ODD | WIDE)
+CHIP_FLIP = {WIDE: 4, EVEN: 1, ODD: 3}
 PART = 96
 PAIR = 2 * PART
 QUAD = 4 * PART
 PARTS = range(3)
-ORDERS = ((ODD, WIDE, EVEN), (EVEN, ODD, WIDE), (WIDE, EVEN, ODD))
+ORDERS = ((WIDE, ODD, EVEN), (EVEN, WIDE, ODD), (ODD, EVEN, WIDE))
 FIRST = 4 * UNIT
 SWAP_LAST = [(i, i ^ 1) for i in range(16)]
 ALONG_Z = [list(range(0, 16, 2)), list(range(1, 16, 2))]
 
 
-SENT = {dim: [] for dim in (EVEN, ODD, WIDE)}
+SENT = {dim: [] for dim in (WIDE, EVEN, ODD)}
 for part_of, (one, two, three) in enumerate(ORDERS):
     SENT[two].append((one, part_of))
     SENT[three] += [(one, part_of), (two, part_of)]
@@ -130,9 +130,9 @@
     out_ref[...] = dot(rows_ref[...], block[...])
 
 
-def second_kernel(rows_ref, even, odd, wide, acc_ref, out_ref, block):
+def second_kernel(rows_ref, wide, even, odd, acc_ref, out_ref, block):
     came = {EVEN: even, ODD: odd, WIDE: wide}
-    for dim in (EVEN, ODD, WIDE):
+    for dim in (WIDE, EVEN, ODD):
         for i, (away, part) in enumerate(SENT[dim]):
             at = rows_of(away | dim, part).start - FIRST
             block[at : at + PART] = came[dim][PART * i : PART * i + PART]
@@ -141,7 +141,7 @@
     out_ref[...] = acc_ref[...] + dot(rows_ref[:, : block.shape[0]], block[...])
 
 
-def third_kernel(rows_ref, even, odd, wide, acc_ref, out_ref, block):
+def third_kernel(rows_ref, wide, even, odd, acc_ref, out_ref, block):
     came = {EVEN: even, ODD: odd, WIDE: wide}
     block[:PART] = jnp.zeros((PART, KVW), BF)
     for part in PARTS:
@@ -308,7 +308,7 @@
     at, weight, rows = lax.optimization_barrier((at, weight, rows))
 
     rows_other = swap(rows)
-    dims = (EVEN, ODD, WIDE)
+    dims = (WIDE, EVEN, ODD)
     near = {dim: flip(weight, dim) for dim in dims}
     kept = turn(at, rows)
     kept_rows = back(kept)

time: 149 us -> 148 us (level)
  starting transfers between devices: 38.7 us -> 37 us
  transfers between devices with their start and end apart: 25 -> 25, of which waited for: 18 -> 16; matrix products, arithmetic and copies ran while one was open for 1% -> 1% of each run, Pallas kernels for 12% -> 12%
where the time goes in v4:
time: 148 us; the launch traced here: 146 us
  waiting for transfers between devices  39.5 us (27%)
  blocking collectives  39.3 us (27%)
  starting transfers between devices  37 us (25%)
  Pallas kernels  23.9 us (16%)
  local copies, waits for them, and re-layouts  2.91 us (2%)
  other arithmetic  2.25 us (2%)
    ppermute x20, starting transfers between devices, flip(): lax.ppermute(value, 'fsdp', [(i, i ^ 2 * CHIP_FLIP[dim]) for i in range(1...  34.8 us
    ppermute x20, waiting for transfers between devices, flip(): lax.ppermute(value, 'fsdp', [(i, i ^ 2 * CHIP_FLIP[dim]) for i in range(1...  34.1 us
    all_to_all x1, blocking collectives, replica_mean(): pieces = lax.all_to_all(delta, 'replica', 0, 0, axis_index_groups=ALONG_Z)  22.9 us
    all_to_all x1, blocking collectives, replica_mean(): return lax.all_to_all(pieces, 'replica', 0, 0, axis_index_groups=ALONG_Z)  16.4 us
    pallas_call x6, Pallas kernels, project(): pl.pallas_call(kernel, grid=(1,), in_specs=[pl.BlockSpec((TOK, width), la...  7.03 us
    pallas_call x5, Pallas kernels, grad_blocks(): pl.pallas_call(kernel, in_specs=[here] * 4, out_specs=[here] * len(groups...  5.75 us
    pallas_call x2, Pallas kernels, turn(): pl.pallas_call(turn_kernel, grid_spec=pltpu.PrefetchScalarGridSpec(num_sc...  5.13 us
    ppermute x1, waiting for transfers between devices, replica_mean(): other = lax.ppermute(part, 'replica', SWAP_LAST)  3.17 us
  transfers between devices with their start and end apart: 25, of which 16 were waited for; matrix products, arithmetic and copies ran while one was open for 1% of the time, Pallas kernels for 12%

profile of v4, /device:TPU:2, one launch (start us, length us, event | category | flops | bytes accessed | tf_op | source)
XLA Modules:
  0.0 146.2 jit_solution(16939722129617713604)
XLA Ops:
  1.1 3.3 %collective-permute-start = (bf16[288,1024]{1,0:T(8,128)(2,1)}, bf16[288,1024]{1,0:T(8,128)(2,1)S(1)}, u32[]{:S(2)}, u32[]{:S(2)}) collective-permute-start(bf16[288,1024]{1,0:T(8,128)(2,1)} %bitcast.18), channel_id=1, source_target_pairs={{0,8},{1,9},{2,10},{3,11},{4,12},{5,13},{6,14},{7,15},{8,0},{9,1},... | collective-permute-start | bytes 1769480 | tf_op jit(solution)/shard_map/ppermute | solution.py:63
  4.9 2.2 %collective-permute-start.2 = (bf16[288,1024]{1,0:T(8,128)(2,1)}, bf16[288,1024]{1,0:T(8,128)(2,1)S(1)}, u32[]{:S(2)}, u32[]{:S(2)}) collective-permute-start(bf16[288,1024]{1,0:T(8,128)(2,1)} %bitcast.20), channel_id=1, source_target_pairs={{0,6},{1,7},{2,4},{3,5},{4,2},{5,3},{6,0},{7,1},{8,14},{9,15},{10,... | collective-permute-start | bytes 1769480 | tf_op jit(solution)/shard_map/ppermute | solution.py:63
  7.1 2.3 %copy-done.1 = bf16[1,512,4608]{2,1,0:T(8,128)(2,1)S(1)} copy-done((bf16[1,512,4608]{2,1,0:T(8,128)(2,1)S(1)}, bf16[1,512,4608]{2,1,0:T(8,128)(2,1)}, u32[]{:S(2)}) %copy-start.1) | copy-done | bytes 4718616
  9.4 2.6 %turn.2.rows_ref.one = bf16[2304,512]{1,0:T(8,128)(2,1)S(1)} custom-call(s32[9]{0:T(128)S(1)} %stack.39.at_ref, bf16[512,4608]{1,0:T(8,128)(2,1)S(1)} %bitcast.25), custom_call_target="tpu_custom_call" | custom-call | bytes 7077888 | tf_op jit(solution)/shard_map/turn/pallas_call | solution.py:88
  12.9 5.6 %collective-permute-done.refs_1_ = bf16[288,1024]{1,0:T(8,128)(2,1)S(1)} collective-permute-done((bf16[288,1024]{1,0:T(8,128)(2,1)}, bf16[288,1024]{1,0:T(8,128)(2,1)S(1)}, u32[]{:S(2)}, u32[]{:S(2)}) %collective-permute-start) | collective-permute-done | bytes 589856 | tf_op jit(solution)/shard_map/ppermute | solution.py:63
  25.1 2.6 %turn.3.rows_ref.two = bf16[2304,512]{1,0:T(8,128)(2,1)S(1)} custom-call(s32[9]{0:T(128)S(1)} %stack.39.at_ref, bf16[512,4608]{1,0:T(8,128)(2,1)S(1)} %collective-permute-done.3.rows_ref), custom_call_target="tpu_custom_call" | custom-call | bytes 7077888 | tf_op jit(solution)/shard_map/turn/pallas_call | solution.py:88
  31.8 5.3 %collective-permute-done.4.wide = bf16[288,1024]{1,0:T(8,128)(2,1)S(1)} collective-permute-done((bf16[288,1024]{1,0:T(8,128)(2,1)S(1)}, bf16[288,1024]{1,0:T(8,128)(2,1)S(1)}, u32[]{:S(2)}, u32[]{:S(2)}) %collective-permute-start.4) | collective-permute-done | bytes 589856 | tf_op jit(solution)/shard_map/ppermute | solution.py:63
  38.2 2.4 %collective-permute-start.7 = (bf16[96,1024]{1,0:T(8,128)(2,1)S(1)}, bf16[96,1024]{1,0:T(8,128)(2,1)S(1)}, u32[]{:S(2)}, u32[]{:S(2)}) collective-permute-start(bf16[96,1024]{1,0:T(8,128)(2,1)S(1)} %slice.63), channel_id=1, source_target_pairs={{0,8},{1,9},{2,10},{3,11},{4,12},{5,13},{6,14},{7,15},{8,0},{9,1},... | collective-permute-start | bytes 589832 | tf_op jit(solution)/shard_map/ppermute | solution.py:63
  57.1 1.8 %collective-permute-start.13 = (bf16[384,1024]{1,0:T(8,128)(2,1)S(1)}, bf16[384,1024]{1,0:T(8,128)(2,1)S(1)}, u32[]{:S(2)}, u32[]{:S(2)}) collective-permute-start(bf16[384,1024]{1,0:T(8,128)(2,1)S(1)} %grad.5), channel_id=1, source_target_pairs={{0,2},{1,3},{2,0},{3,1},{4,6},{5,7},{6,4},{7,5},{8,10},{9,11},{10,... | collective-permute-start | bytes 2359304 | tf_op jit(solution)/shard_map/ppermute | solution.py:63
  61.0 2.8 %collective-permute-start.15 = (bf16[192,1024]{1,0:T(8,128)(2,1)S(1)}, bf16[192,1024]{1,0:T(8,128)(2,1)S(1)}, u32[]{:S(2)}, u32[]{:S(2)}) collective-permute-start(bf16[192,1024]{1,0:T(8,128)(2,1)S(1)} %get-tuple-element.68), channel_id=1, source_target_pairs={{0,8},{1,9},{2,10},{3,11},{4,12},{5,13},{6,14},{7,15},{8,0},{9,1},... | collective-permute-start | bytes 1179656 | tf_op jit(solution)/shard_map/ppermute | solution.py:63
  65.8 2.6 %collective-permute-done.19 = bf16[192,1024]{1,0:T(8,128)(2,1)S(1)} collective-permute-done((bf16[192,1024]{1,0:T(8,128)(2,1)S(1)}, bf16[192,1024]{1,0:T(8,128)(2,1)S(1)}, u32[]{:S(2)}, u32[]{:S(2)}) %collective-permute-start.19) | collective-permute-done | bytes 393248 | tf_op jit(solution)/shard_map/ppermute | solution.py:63
  68.5 1.8 %collective-permute-start.20 = (bf16[192,1024]{1,0:T(8,128)(2,1)S(1)}, bf16[192,1024]{1,0:T(8,128)(2,1)S(1)}, u32[]{:S(2)}, u32[]{:S(2)}) collective-permute-start(bf16[192,1024]{1,0:T(8,128)(2,1)S(1)} %add_convert_fusion), channel_id=1, source_target_pairs={{0,2},{1,3},{2,0},{3,1},{4,6},{5,7},{6,4},{7,5},{8,10},{9,11},{10,... | collective-permute-start | bytes 1179656 | tf_op jit(solution)/shard_map/ppermute | solution.py:63
  72.1 2.4 %collective-permute-start.18 = (bf16[192,1024]{1,0:T(8,128)(2,1)S(1)}, bf16[192,1024]{1,0:T(8,128)(2,1)S(1)}, u32[]{:S(2)}, u32[]{:S(2)}) collective-permute-start(bf16[192,1024]{1,0:T(8,128)(2,1)S(1)} %add_convert_fusion.1), channel_id=1, source_target_pairs={{0,8},{1,9},{2,10},{3,11},{4,12},{5,13},{6,14},{7,15},{8,0},{9,1},... | collective-permute-start | bytes 1179656 | tf_op jit(solution)/shard_map/ppermute | solution.py:63
  74.5 3.1 %collective-permute-done.13 = bf16[384,1024]{1,0:T(8,128)(2,1)S(1)} collective-permute-done((bf16[384,1024]{1,0:T(8,128)(2,1)S(1)}, bf16[384,1024]{1,0:T(8,128)(2,1)S(1)}, u32[]{:S(2)}, u32[]{:S(2)}) %collective-permute-start.13) | collective-permute-done | bytes 786464 | tf_op jit(solution)/shard_map/ppermute | solution.py:63
  81.6 3.3 %collective-permute-done.20 = bf16[192,1024]{1,0:T(8,128)(2,1)S(1)} collective-permute-done((bf16[192,1024]{1,0:T(8,128)(2,1)S(1)}, bf16[192,1024]{1,0:T(8,128)(2,1)S(1)}, u32[]{:S(2)}, u32[]{:S(2)}) %collective-permute-start.20) | collective-permute-done | bytes 393248 | tf_op jit(solution)/shard_map/ppermute | solution.py:63
  85.1 1.8 %collective-permute-start.23 = (bf16[96,1024]{1,0:T(8,128)(2,1)S(1)}, bf16[96,1024]{1,0:T(8,128)(2,1)S(1)}, u32[]{:S(2)}, u32[]{:S(2)}) collective-permute-start(bf16[96,1024]{1,0:T(8,128)(2,1)S(1)} %slice.86), channel_id=1, source_target_pairs={{0,6},{1,7},{2,4},{3,5},{4,2},{5,3},{6,0},{7,1},{8,14},{9,15},{10,... | collective-permute-start | bytes 589832 | tf_op jit(solution)/shard_map/ppermute | solution.py:63
  87.1 1.9 %collective-permute-start.22 = (bf16[96,1024]{1,0:T(8,128)(2,1)S(1)}, bf16[96,1024]{1,0:T(8,128)(2,1)S(1)}, u32[]{:S(2)}, u32[]{:S(2)}) collective-permute-start(bf16[96,1024]{1,0:T(8,128)(2,1)S(1)} %slice.87), channel_id=1, source_target_pairs={{0,2},{1,3},{2,0},{3,1},{4,6},{5,7},{6,4},{7,5},{8,10},{9,11},{10,... | collective-permute-start | bytes 589832 | tf_op jit(solution)/shard_map/ppermute | solution.py:63
  90.9 2.5 %collective-permute-start.21 = (bf16[96,1024]{1,0:T(8,128)(2,1)S(1)}, bf16[96,1024]{1,0:T(8,128)(2,1)S(1)}, u32[]{:S(2)}, u32[]{:S(2)}) collective-permute-start(bf16[96,1024]{1,0:T(8,128)(2,1)S(1)} %slice.88), channel_id=1, source_target_pairs={{0,8},{1,9},{2,10},{3,11},{4,12},{5,13},{6,14},{7,15},{8,0},{9,1},... | collective-permute-start | bytes 589832 | tf_op jit(solution)/shard_map/ppermute | solution.py:63
  93.5 4.7 %collective-permute-done.21.refs_3_ = bf16[96,1024]{1,0:T(8,128)(2,1)S(1)} collective-permute-done((bf16[96,1024]{1,0:T(8,128)(2,1)S(1)}, bf16[96,1024]{1,0:T(8,128)(2,1)S(1)}, u32[]{:S(2)}, u32[]{:S(2)}) %collective-permute-start.21) | collective-permute-done | bytes 196640 | tf_op jit(solution)/shard_map/ppermute | solution.py:63
  98.2 2.2 %inner.1 = (f32[288,1024]{1,0:T(8,128)}, f32[288,1024]{1,0:T(8,128)}, bf16[288,1024]{1,0:T(8,128)(2,1)S(1)}, bf16[8,288,128]{2,1,0:T(8,128)(2,1)S(1)}) custom-call(f32[96,1024]{1,0:T(8,128)S(1)} %slice.76.refs_0_, f32[96,1024]{1,0:T(8,128)S(1)} %slice.77.refs_1_, f32[96,1024]{1,0:T(8,128)S(1)} %slice.78.refs_2_, ...), custom_call_target="tpu_custom_call" | custom-call | flops 5898240 | bytes 9437184 | tf_op jit(solution)/shard_map/inner/pallas_call | solution.py:224
  100.4 22.9 %all_to_all.10.parts_ref = bf16[8,288,128]{2,1,0:T(8,128)(2,1)S(1)} all-to-all(bf16[8,288,128]{2,1,0:T(8,128)(2,1)S(1)} %get-tuple-element.82), channel_id=1, replica_groups={{0,32,64,96,128,160,192,224},{16,48,80,112,144,176,208,240},{1,33,65,97..., dimensions={0} | all-to-all | bytes 1179648 | tf_op jit(solution)/shard_map/all_to_all | solution.py:256
  124.7 3.2 %collective-permute-done.24 = bf16[288,128]{1,0:T(8,128)(2,1)S(1)} collective-permute-done((bf16[288,128]{1,0:T(8,128)(2,1)S(1)}, bf16[288,128]{1,0:T(8,128)(2,1)S(1)}, u32[]{:S(2)}, u32[]{:S(2)}) %collective-permute-start.24) | collective-permute-done | bytes 73760 | tf_op jit(solution)/shard_map/ppermute | solution.py:258
  128.0 16.4 %all_to_all.11.mean_ref = bf16[8,288,128]{2,1,0:T(8,128)(2,1)S(1)} all-to-all(bf16[8,288,128]{2,1,0:T(8,128)(2,1)S(1)} %broadcast_in_dim.15), channel_id=1, replica_groups={{0,32,64,96,128,160,192,224},{16,48,80,112,144,176,208,240},{1,33,65,97..., dimensions={0} | all-to-all | bytes 1179648 | tf_op jit(solution)/shard_map/all_to_all | solution.py:261
  144.4 1.8 %outer.1 = (bf16[288,1024]{1,0:T(8,128)(2,1)}, f32[288,1024]{1,0:T(8,128)}, f32[288,1024]{1,0:T(8,128)}) custom-call(bf16[8,288,128]{2,1,0:T(8,128)(2,1)S(1)} %all_to_all.11.mean_ref, bf16[288,1024]{1,0:T(8,128)(2,1)S(1)} %get-tuple-element.83.w_ref, f32[288,1024]{1,0:T(8,128)S(1)} %copy-done.2, f32[288,1024]{1,0:T(8,128)S(1)} %copy-done.3), custom_call_target="tpu_custom_call" | custom-call | flops 2359296 | bytes 7340032 | tf_op jit(solution)/shard_map/outer/pallas_call | solution.py:282
  (87 shorter events, 43.4 us)
Async XLA Ops:
  1.0 19.6 %collective-permute-start.3 = (bf16[512,4608]{1,0:T(8,128)(2,1)}, bf16[512,4608]{1,0:T(8,128)(2,1)S(1)}, u32[]{:S(2)}, u32[]{:S(2)}) collective-permute-start(bf16[512,4608]{1,0:T(8,128)(2,1)} %bitcast.24), channel_id=1, source_target_pairs={{0,1},{1,0},{2,3},{3,2},{4,5},{5,4},{6,7},{7,6},{8,9},{9,8},{10,11... | collective-permute-start | bytes 14155784 | tf_op jit(solution)/shard_map/ppermute | solution.py:67
  1.1 17.5 %collective-permute-start = (bf16[288,1024]{1,0:T(8,128)(2,1)}, bf16[288,1024]{1,0:T(8,128)(2,1)S(1)}, u32[]{:S(2)}, u32[]{:S(2)}) collective-permute-start(bf16[288,1024]{1,0:T(8,128)(2,1)} %bitcast.18), channel_id=1, source_target_pairs={{0,8},{1,9},{2,10},{3,11},{4,12},{5,13},{6,14},{7,15},{8,0},{9,1},... | collective-permute-start | bytes 1769480 | tf_op jit(solution)/shard_map/ppermute | solution.py:63
  4.4 15.6 %collective-permute-start.1 = (bf16[288,1024]{1,0:T(8,128)(2,1)}, bf16[288,1024]{1,0:T(8,128)(2,1)S(1)}, u32[]{:S(2)}, u32[]{:S(2)}) collective-permute-start(bf16[288,1024]{1,0:T(8,128)(2,1)} %bitcast.19), channel_id=1, source_target_pairs={{0,2},{1,3},{2,0},{3,1},{4,6},{5,7},{6,4},{7,5},{8,10},{9,11},{10,... | collective-permute-start | bytes 1769480 | tf_op jit(solution)/shard_map/ppermute | solution.py:63
  4.9 15.8 %collective-permute-start.2 = (bf16[288,1024]{1,0:T(8,128)(2,1)}, bf16[288,1024]{1,0:T(8,128)(2,1)S(1)}, u32[]{:S(2)}, u32[]{:S(2)}) collective-permute-start(bf16[288,1024]{1,0:T(8,128)(2,1)} %bitcast.20), channel_id=1, source_target_pairs={{0,6},{1,7},{2,4},{3,5},{4,2},{5,3},{6,0},{7,1},{8,14},{9,15},{10,... | collective-permute-start | bytes 1769480 | tf_op jit(solution)/shard_map/ppermute | solution.py:63
  7.1 39.3 %collective-permute-start.10 = (bf16[512,1024]{1,0:T(8,128)(2,1)}, bf16[512,1024]{1,0:T(8,128)(2,1)S(1)}, u32[]{:S(2)}, u32[]{:S(2)}) collective-permute-start(bf16[512,1024]{1,0:T(8,128)(2,1)} %bitcast.28), channel_id=1, source_target_pairs={{0,1},{1,0},{2,3},{3,2},{4,5},{5,4},{6,7},{7,6},{8,9},{9,8},{10,11... | collective-permute-start | bytes 3145736 | tf_op jit(solution)/shard_map/ppermute | solution.py:67
  21.0 16.1 %collective-permute-start.4 = (bf16[288,1024]{1,0:T(8,128)(2,1)S(1)}, bf16[288,1024]{1,0:T(8,128)(2,1)S(1)}, u32[]{:S(2)}, u32[]{:S(2)}) collective-permute-start(bf16[288,1024]{1,0:T(8,128)(2,1)S(1)} %get-tuple-element.96), channel_id=1, source_target_pairs={{0,8},{1,9},{2,10},{3,11},{4,12},{5,13},{6,14},{7,15},{8,0},{9,1},... | collective-permute-start | bytes 1769480 | tf_op jit(solution)/shard_map/ppermute | solution.py:63
  22.7 14.4 %collective-permute-start.5 = (bf16[288,1024]{1,0:T(8,128)(2,1)S(1)}, bf16[288,1024]{1,0:T(8,128)(2,1)S(1)}, u32[]{:S(2)}, u32[]{:S(2)}) collective-permute-start(bf16[288,1024]{1,0:T(8,128)(2,1)S(1)} %get-tuple-element.97), channel_id=1, source_target_pairs={{0,2},{1,3},{2,0},{3,1},{4,6},{5,7},{6,4},{7,5},{8,10},{9,11},{10,... | collective-permute-start | bytes 1769480 | tf_op jit(solution)/shard_map/ppermute | solution.py:63
  24.2 14.0 %collective-permute-start.6 = (bf16[288,1024]{1,0:T(8,128)(2,1)S(1)}, bf16[288,1024]{1,0:T(8,128)(2,1)S(1)}, u32[]{:S(2)}, u32[]{:S(2)}) collective-permute-start(bf16[288,1024]{1,0:T(8,128)(2,1)S(1)} %get-tuple-element.95), channel_id=1, source_target_pairs={{0,6},{1,7},{2,4},{3,5},{4,2},{5,3},{6,0},{7,1},{8,14},{9,15},{10,... | collective-permute-start | bytes 1769480 | tf_op jit(solution)/shard_map/ppermute | solution.py:63
  38.2 8.2 %collective-permute-start.7 = (bf16[96,1024]{1,0:T(8,128)(2,1)S(1)}, bf16[96,1024]{1,0:T(8,128)(2,1)S(1)}, u32[]{:S(2)}, u32[]{:S(2)}) collective-permute-start(bf16[96,1024]{1,0:T(8,128)(2,1)S(1)} %slice.63), channel_id=1, source_target_pairs={{0,8},{1,9},{2,10},{3,11},{4,12},{5,13},{6,14},{7,15},{8,0},{9,1},... | collective-permute-start | bytes 589832 | tf_op jit(solution)/shard_map/ppermute | solution.py:63
  40.6 5.8 %collective-permute-start.8 = (bf16[96,1024]{1,0:T(8,128)(2,1)S(1)}, bf16[96,1024]{1,0:T(8,128)(2,1)S(1)}, u32[]{:S(2)}, u32[]{:S(2)}) collective-permute-start(bf16[96,1024]{1,0:T(8,128)(2,1)S(1)} %slice.64), channel_id=1, source_target_pairs={{0,2},{1,3},{2,0},{3,1},{4,6},{5,7},{6,4},{7,5},{8,10},{9,11},{10,... | collective-permute-start | bytes 589832 | tf_op jit(solution)/shard_map/ppermute | solution.py:63
  42.2 5.8 %collective-permute-start.9 = (bf16[96,1024]{1,0:T(8,128)(2,1)S(1)}, bf16[96,1024]{1,0:T(8,128)(2,1)S(1)}, u32[]{:S(2)}, u32[]{:S(2)}) collective-permute-start(bf16[96,1024]{1,0:T(8,128)(2,1)S(1)} %slice.65), channel_id=1, source_target_pairs={{0,6},{1,7},{2,4},{3,5},{4,2},{5,3},{6,0},{7,1},{8,14},{9,15},{10,... | collective-permute-start | bytes 589832 | tf_op jit(solution)/shard_map/ppermute | solution.py:63
  49.7 3.4 %collective-permute-start.12 = (bf16[512,1024]{1,0:T(8,128)(2,1)S(1)}, bf16[512,1024]{1,0:T(8,128)(2,1)S(1)}, u32[]{:S(2)}, u32[]{:S(2)}) collective-permute-start(bf16[512,1024]{1,0:T(8,128)(2,1)S(1)} %third_kernel.2), channel_id=1, source_target_pairs={{0,1},{1,0},{2,3},{3,2},{4,5},{5,4},{6,7},{7,6},{8,9},{9,8},{10,11... | collective-permute-start | bytes 3145736 | tf_op jit(solution)/shard_map/ppermute | solution.py:67
  54.8 13.6 %collective-permute-start.19 = (bf16[192,1024]{1,0:T(8,128)(2,1)S(1)}, bf16[192,1024]{1,0:T(8,128)(2,1)S(1)}, u32[]{:S(2)}, u32[]{:S(2)}) collective-permute-start(bf16[192,1024]{1,0:T(8,128)(2,1)S(1)} %get-tuple-element.81), channel_id=1, source_target_pairs={{0,8},{1,9},{2,10},{3,11},{4,12},{5,13},{6,14},{7,15},{8,0},{9,1},... | collective-permute-start | bytes 1179656 | tf_op jit(solution)/shard_map/ppermute | solution.py:63
  57.1 20.5 %collective-permute-start.13 = (bf16[384,1024]{1,0:T(8,128)(2,1)S(1)}, bf16[384,1024]{1,0:T(8,128)(2,1)S(1)}, u32[]{:S(2)}, u32[]{:S(2)}) collective-permute-start(bf16[384,1024]{1,0:T(8,128)(2,1)S(1)} %grad.5), channel_id=1, source_target_pairs={{0,2},{1,3},{2,0},{3,1},{4,6},{5,7},{6,4},{7,5},{8,10},{9,11},{10,... | collective-permute-start | bytes 2359304 | tf_op jit(solution)/shard_map/ppermute | solution.py:63
  59.9 12.1 %collective-permute-start.17 = (bf16[192,1024]{1,0:T(8,128)(2,1)S(1)}, bf16[192,1024]{1,0:T(8,128)(2,1)S(1)}, u32[]{:S(2)}, u32[]{:S(2)}) collective-permute-start(bf16[192,1024]{1,0:T(8,128)(2,1)S(1)} %get-tuple-element.77), channel_id=1, source_target_pairs={{0,6},{1,7},{2,4},{3,5},{4,2},{5,3},{6,0},{7,1},{8,14},{9,15},{10,... | collective-permute-start | bytes 1179656 | tf_op jit(solution)/shard_map/ppermute | solution.py:63
  61.0 16.6 %collective-permute-start.15 = (bf16[192,1024]{1,0:T(8,128)(2,1)S(1)}, bf16[192,1024]{1,0:T(8,128)(2,1)S(1)}, u32[]{:S(2)}, u32[]{:S(2)}) collective-permute-start(bf16[192,1024]{1,0:T(8,128)(2,1)S(1)} %get-tuple-element.68), channel_id=1, source_target_pairs={{0,8},{1,9},{2,10},{3,11},{4,12},{5,13},{6,14},{7,15},{8,0},{9,1},... | collective-permute-start | bytes 1179656 | tf_op jit(solution)/shard_map/ppermute | solution.py:63
  63.8 15.2 %collective-permute-start.14 = (bf16[192,1024]{1,0:T(8,128)(2,1)S(1)}, bf16[192,1024]{1,0:T(8,128)(2,1)S(1)}, u32[]{:S(2)}, u32[]{:S(2)}) collective-permute-start(bf16[192,1024]{1,0:T(8,128)(2,1)S(1)} %get-tuple-element.67), channel_id=1, source_target_pairs={{0,6},{1,7},{2,4},{3,5},{4,2},{5,3},{6,0},{7,1},{8,14},{9,15},{10,... | collective-permute-start | bytes 1179656 | tf_op jit(solution)/shard_map/ppermute | solution.py:63
  68.5 16.4 %collective-permute-start.20 = (bf16[192,1024]{1,0:T(8,128)(2,1)S(1)}, bf16[192,1024]{1,0:T(8,128)(2,1)S(1)}, u32[]{:S(2)}, u32[]{:S(2)}) collective-permute-start(bf16[192,1024]{1,0:T(8,128)(2,1)S(1)} %add_convert_fusion), channel_id=1, source_target_pairs={{0,2},{1,3},{2,0},{3,1},{4,6},{5,7},{6,4},{7,5},{8,10},{9,11},{10,... | collective-permute-start | bytes 1179656 | tf_op jit(solution)/shard_map/ppermute | solution.py:63
  72.1 14.8 %collective-permute-start.18 = (bf16[192,1024]{1,0:T(8,128)(2,1)S(1)}, bf16[192,1024]{1,0:T(8,128)(2,1)S(1)}, u32[]{:S(2)}, u32[]{:S(2)}) collective-permute-start(bf16[192,1024]{1,0:T(8,128)(2,1)S(1)} %add_convert_fusion.1), channel_id=1, source_target_pairs={{0,8},{1,9},{2,10},{3,11},{4,12},{5,13},{6,14},{7,15},{8,0},{9,1},... | collective-permute-start | bytes 1179656 | tf_op jit(solution)/shard_map/ppermute | solution.py:63
  79.1 11.6 %collective-permute-start.16 = (bf16[192,1024]{1,0:T(8,128)(2,1)S(1)}, bf16[192,1024]{1,0:T(8,128)(2,1)S(1)}, u32[]{:S(2)}, u32[]{:S(2)}) collective-permute-start(bf16[192,1024]{1,0:T(8,128)(2,1)S(1)} %add_convert_fusion.2), channel_id=1, source_target_pairs={{0,6},{1,7},{2,4},{3,5},{4,2},{5,3},{6,0},{7,1},{8,14},{9,15},{10,... | collective-permute-start | bytes 1179656 | tf_op jit(solution)/shard_map/ppermute | solution.py:63
  85.1 8.4 %collective-permute-start.23 = (bf16[96,1024]{1,0:T(8,128)(2,1)S(1)}, bf16[96,1024]{1,0:T(8,128)(2,1)S(1)}, u32[]{:S(2)}, u32[]{:S(2)}) collective-permute-start(bf16[96,1024]{1,0:T(8,128)(2,1)S(1)} %slice.86), channel_id=1, source_target_pairs={{0,6},{1,7},{2,4},{3,5},{4,2},{5,3},{6,0},{7,1},{8,14},{9,15},{10,... | collective-permute-start | bytes 589832 | tf_op jit(solution)/shard_map/ppermute | solution.py:63
  87.1 6.4 %collective-permute-start.22 = (bf16[96,1024]{1,0:T(8,128)(2,1)S(1)}, bf16[96,1024]{1,0:T(8,128)(2,1)S(1)}, u32[]{:S(2)}, u32[]{:S(2)}) collective-permute-start(bf16[96,1024]{1,0:T(8,128)(2,1)S(1)} %slice.87), channel_id=1, source_target_pairs={{0,2},{1,3},{2,0},{3,1},{4,6},{5,7},{6,4},{7,5},{8,10},{9,11},{10,... | collective-permute-start | bytes 589832 | tf_op jit(solution)/shard_map/ppermute | solution.py:63
  90.9 7.3 %collective-permute-start.21 = (bf16[96,1024]{1,0:T(8,128)(2,1)S(1)}, bf16[96,1024]{1,0:T(8,128)(2,1)S(1)}, u32[]{:S(2)}, u32[]{:S(2)}) collective-permute-start(bf16[96,1024]{1,0:T(8,128)(2,1)S(1)} %slice.88), channel_id=1, source_target_pairs={{0,8},{1,9},{2,10},{3,11},{4,12},{5,13},{6,14},{7,15},{8,0},{9,1},... | collective-permute-start | bytes 589832 | tf_op jit(solution)/shard_map/ppermute | solution.py:63
  123.5 4.4 %collective-permute-start.24 = (bf16[288,128]{1,0:T(8,128)(2,1)S(1)}, bf16[288,128]{1,0:T(8,128)(2,1)S(1)}, u32[]{:S(2)}, u32[]{:S(2)}) collective-permute-start(bf16[288,128]{1,0:T(8,128)(2,1)S(1)} %totals.1), channel_id=1, source_target_pairs={{0,16},{16,0},{32,48},{48,32},{64,80},{80,64},{96,112},{112,96},{1... | collective-permute-start | bytes 221192 | tf_op jit(solution)/shard_map/ppermute | solution.py:258
  (10 other events, 57.5 us)
